TPU v7x, 256 devices: a whole 4x4x8 slice. The times are simulated.
256 devices in a mesh: scan: 8 (over x, core), brick: 32 (over z, y).
Axes of the slice: x: 4, y: 4, z: 8, core: 2. Of those that a mesh axis runs over, the one named last changes fastest.
Arguments:
- features: bfloat16 [8, 32, 64, 4096], P('scan', 'brick'), may hold values from -6 to 6
- cotangent: bfloat16 [8, 32, 64, 4096], P('scan', 'brick'), may hold values from -6 to 6
- weight: bfloat16 [27, 64, 64], replicated, may hold values from -0.15625 to 0.15625
- neighbours: int32 [8, 32, 27], P('scan', 'brick'), may hold values from -1 to 31, as said below
- occupancy: int32 [8, 32, 4096], P('scan', 'brick'), may hold values 0 or 1
Outputs:
- output: bfloat16 [8, 32, 64, 4096], P('scan', 'brick')
- grad_input: bfloat16 [8, 32, 64, 4096], P('scan', 'brick')
- grad_weight: float32 [27, 64, 64], replicated
Inputs may be any that keep to these rules, and one draw needn't show every extreme that they name: `neighbours`: entry k = 9 (dz + 1) + 3 (dy + 1) + (dx + 1) of brick g names the occupied brick of the same scan at brick offset (dz, dy, dx), or -1; entry 13 is g. Bricks g lie in layer g // 1 of brick positions, so a neighbour at offset dz is one of the bricks of layer g + dz. The relation is symmetric.
All inputs are finite; a program needn't handle non-finite values. No bound on the sum of `occupancy` on one device may be relied on, other than what follows from the above.
Results may differ from a plain program's by a relative error of at most 0.001.
Values may be sent and summed in bfloat16 or wider, within the bound.
A program may use at most 256 MiB of HBM per device.

v0:
```python
import jax
import jax.numpy as jnp
from jax import lax
from jax.sharding import PartitionSpec as P

BS = 16
BD = 1


def with_halo(array, sides, width):
    for axis, dim in sides:
        count, length = (lax.axis_size(axis), array.shape[dim])
        up = [(i, (i + 1) % count) for i in range(count - 1)]
        down = [(j, i) for i, j in up]
        last = lax.slice_in_dim(array, length - width, length, axis=dim)
        leading = lax.slice_in_dim(array, 0, width, axis=dim)
        before = lax.ppermute(last, axis, up)
        after = lax.ppermute(leading, axis, down)
        array = jnp.concatenate([before, array, after], axis=dim)
    return array


def assemble(lower_pool, own_pool, upper_pool, offset_rows, valid_rows):
    layer_parts = []
    for shift_z in (-1, 0, 1):
        source_pool = (lower_pool, own_pool, upper_pool)[shift_z + 1]
        plane_parts = []
        for shift_y in (-1, 0, 1):
            columns = []
            for shift_x in (-1, 0, 1):
                k = 9 * (shift_z + 1) + 3 * (shift_y + 1) + (shift_x + 1)
                y_part = (slice(BS - 1, BS), slice(0, BS), slice(0, 1))[shift_y + 1]
                x_part = (slice(BS - 1, BS), slice(0, BS), slice(0, 1))[shift_x + 1]
                portion = source_pool[:, :, :, y_part, x_part]
                fetched = jnp.take(portion, offset_rows[:, k], axis=0)
                fetched = jnp.where(
                    valid_rows[:, k][:, None, None, None, None], fetched, jnp.zeros_like(fetched)
                )
                columns.append(fetched)
            plane_parts.append(jnp.concatenate(columns, axis=4))
        layer_parts.append(jnp.concatenate(plane_parts, axis=3))
    return jnp.concatenate(layer_parts, axis=2)


def stacked_block(padded, plane_start, depth, sign):
    pieces = []
    for k in range(27):
        start_z = plane_start + 1 + sign * (k // 9 - 1)
        start_y = 1 + sign * (k // 3 % 3 - 1)
        start_x = 1 + sign * (k % 3 - 1)
        pieces.append(
            padded[:, :, start_z : start_z + depth, start_y : start_y + BS, start_x : start_x + BS]
        )
    joined = jnp.stack(pieces, axis=1)
    return joined.reshape(padded.shape[0], 27 * padded.shape[1], depth * BS * BS)


def neighbour_pools(fields):
    channels = fields.shape[1]
    own_cube = fields.reshape(BD, channels, BS, BS, BS)
    extended = with_halo(fields, (("brick", 0),), BD)
    ext_cube = extended.reshape(3 * BD, channels, BS, BS, BS)
    lower_pool = ext_cube[:BD, :, BS - 1 : BS]
    upper_pool = ext_cube[2 * BD :, :, 0:1]
    return (lower_pool, own_cube, upper_pool)


def local(features, cotangent, weight, neighbours, occupancy):
    device = lax.axis_index("brick")
    voxel_mask = occupancy[0].astype(jnp.bfloat16)[:, None, :]
    float_mask = voxel_mask.astype(jnp.float32)
    brick_ids = neighbours[0]
    valid_rows = brick_ids >= 0
    layer_step = jnp.arange(27) // 9 - 1
    offset_rows = brick_ids - (device + layer_step[None, :]) * BD
    offset_rows = jnp.where(valid_rows, offset_rows, 0)
    live_feat = features[0] * voxel_mask
    upstream = cotangent[0] * voxel_mask
    channels = live_feat.shape[1]
    lower_pool, own_cube, upper_pool = neighbour_pools(live_feat)
    lower_grad, own_grad, upper_grad = neighbour_pools(upstream)
    padded = assemble(lower_pool, own_cube, upper_pool, offset_rows, valid_rows)
    up_padded = assemble(lower_grad, own_grad, upper_grad, offset_rows, valid_rows)
    forward_matrix = jnp.transpose(weight, (1, 0, 2)).reshape(channels, 27 * channels)
    backward_matrix = jnp.transpose(weight, (2, 0, 1)).reshape(channels, 27 * channels)
    depth = 2
    block_voxels = depth * BS * BS
    out_blocks = []
    grad_blocks = []
    weight_terms = jnp.zeros((channels, 27 * channels), jnp.float32)
    for block in range(BS // depth):
        plane_start = block * depth
        forward_stack = stacked_block(padded, plane_start, depth, 1)
        out_blocks.append(
            jnp.einsum(
                "om,bmv->bov", forward_matrix, forward_stack, preferred_element_type=jnp.float32
            )
        )
        backward_stack = stacked_block(up_padded, plane_start, depth, -1)
        grad_blocks.append(
            jnp.einsum(
                "om,bmv->bov", backward_matrix, backward_stack, preferred_element_type=jnp.float32
            )
        )
        up_block = upstream[:, :, plane_start * BS * BS : plane_start * BS * BS + block_voxels]
        weight_terms = weight_terms + jnp.einsum(
            "bov,bmv->om", up_block, forward_stack, preferred_element_type=jnp.float32
        )
    output = (jnp.concatenate(out_blocks, axis=2) * float_mask).astype(jnp.bfloat16)
    grad_input = (jnp.concatenate(grad_blocks, axis=2) * float_mask).astype(jnp.bfloat16)
    partial_weight = jnp.transpose(weight_terms.reshape(channels, 27, channels), (1, 0, 2))
    grad_weight = lax.psum(partial_weight, ("scan", "brick"))
    return (output[None], grad_input[None], grad_weight)


def solution(mesh):
    in_specs = (
        P("scan", "brick", None, None),
        P("scan", "brick", None, None),
        P(),
        P("scan", "brick", None),
        P("scan", "brick", None),
    )
    out_specs = (P("scan", "brick", None, None), P("scan", "brick", None, None), P())
    return jax.shard_map(local, mesh=mesh, in_specs=in_specs, out_specs=out_specs, check_vma=False)
```

profile of v0, /device:TPU:1, one launch (start us, length us, event | category | flops | bytes accessed | tf_op | source)
XLA Modules:
  0.0 597.5 jit_solution(42658681427627676)
XLA Ops:
  8.0 2.2 bitcast_multiply_fusion
  10.3 4.8 collective-permute-start
  17.7 5.5 collective-permute-start.2
  27.1 2.4 copy.43
  64.9 2.6 select_select_fusion
  67.5 3.1 broadcast_select_fusion.31
  70.6 2.5 broadcast_select_fusion.30
  95.9 3.0 maximum_maximum_fusion.3
  103.8 2.4 constant_dynamic-update-slice_fusion.403
  106.3 2.1 constant_dynamic-update-slice_fusion.402
  110.4 3.5 maximum_maximum_fusion.1
  113.9 2.4 copy.31
  119.8 2.1 broadcast_select_fusion.39
  121.9 3.3 broadcast_select_fusion.71
  133.2 2.4 copy.44
  135.7 3.0 broadcast_select_fusion.38
  164.0 2.6 fusion.112
  168.9 4.6 broadcast_select_fusion.70
  173.9 6.2 %copy.35 = bf16[1,27,64,2,16,16]{2,1,5,4,3,0:T(8,128)(2,1)} copy(bf16[1,27,64,2,16,16]{2,5,4,3,1,0:T(8,128)(2,1)S(1)} %get-tuple-element.210) | data formatting | bytes 3538944 | tf_op jit(solution)/shard_map/stack | solution.py:54
  180.1 6.4 %reshape.1525 = bf16[1728,512]{0,1:T(8,128)(2,1)} reshape(bf16[1,27,64,2,16,16]{2,1,5,4,3,0:T(8,128)(2,1)} %copy.35) | data formatting | bytes 3538944 | tf_op jit(solution)/shard_map/reshape.110
  186.4 8.0 %copy.33 = bf16[1,27,64,2,16,16]{2,1,5,4,3,0:T(8,128)(2,1)} copy(bf16[1,27,64,2,16,16]{2,5,4,3,1,0:T(8,128)(2,1)} %get-tuple-element.152) | data formatting | bytes 3538944 | tf_op jit(solution)/shard_map/stack | solution.py:54
  194.4 6.7 %reshape.1523 = bf16[1728,512]{0,1:T(8,128)(2,1)} reshape(bf16[1,27,64,2,16,16]{2,1,5,4,3,0:T(8,128)(2,1)} %copy.33) | data formatting | bytes 3538944 | tf_op jit(solution)/shard_map/reshape.108
  201.2 8.0 %copy.36 = bf16[1,27,64,2,16,16]{2,1,5,4,3,0:T(8,128)(2,1)} copy(bf16[1,27,64,2,16,16]{2,5,4,3,1,0:T(8,128)(2,1)} %copy-done.32) | data formatting | bytes 3538944 | tf_op jit(solution)/shard_map/stack | solution.py:54
  209.2 6.4 %reshape.1526 = bf16[1728,512]{0,1:T(8,128)(2,1)} reshape(bf16[1,27,64,2,16,16]{2,1,5,4,3,0:T(8,128)(2,1)} %copy.36) | data formatting | bytes 3538944 | tf_op jit(solution)/shard_map/reshape.112
  215.5 8.0 %copy.37 = bf16[1,27,64,2,16,16]{2,1,5,4,3,0:T(8,128)(2,1)} copy(bf16[1,27,64,2,16,16]{2,5,4,3,1,0:T(8,128)(2,1)} %copy-done.31) | data formatting | bytes 3538944 | tf_op jit(solution)/shard_map/stack | solution.py:54
  223.5 6.5 %reshape.1527 = bf16[1728,512]{0,1:T(8,128)(2,1)} reshape(bf16[1,27,64,2,16,16]{2,1,5,4,3,0:T(8,128)(2,1)} %copy.37) | data formatting | bytes 3538944 | tf_op jit(solution)/shard_map/reshape.114
  230.0 8.0 %copy.38 = bf16[1,27,64,2,16,16]{2,1,5,4,3,0:T(8,128)(2,1)} copy(bf16[1,27,64,2,16,16]{2,5,4,3,1,0:T(8,128)(2,1)} %copy-done.30) | data formatting | bytes 3538944 | tf_op jit(solution)/shard_map/stack | solution.py:54
  238.0 6.4 %reshape.1528 = bf16[1728,512]{0,1:T(8,128)(2,1)} reshape(bf16[1,27,64,2,16,16]{2,1,5,4,3,0:T(8,128)(2,1)} %copy.38) | data formatting | bytes 3538944 | tf_op jit(solution)/shard_map/reshape.116
  244.4 8.0 %copy.39 = bf16[1,27,64,2,16,16]{2,1,5,4,3,0:T(8,128)(2,1)} copy(bf16[1,27,64,2,16,16]{2,5,4,3,1,0:T(8,128)(2,1)} %copy-done.29) | data formatting | bytes 3538944 | tf_op jit(solution)/shard_map/stack | solution.py:54
  252.4 6.5 %reshape.1529 = bf16[1728,512]{0,1:T(8,128)(2,1)} reshape(bf16[1,27,64,2,16,16]{2,1,5,4,3,0:T(8,128)(2,1)} %copy.39) | data formatting | bytes 3538944 | tf_op jit(solution)/shard_map/reshape.118
  258.9 8.0 %copy.40 = bf16[1,27,64,2,16,16]{2,1,5,4,3,0:T(8,128)(2,1)} copy(bf16[1,27,64,2,16,16]{2,5,4,3,1,0:T(8,128)(2,1)} %copy-done.28) | data formatting | bytes 3538944 | tf_op jit(solution)/shard_map/stack | solution.py:54
  266.9 6.4 %reshape.1530 = bf16[1728,512]{0,1:T(8,128)(2,1)} reshape(bf16[1,27,64,2,16,16]{2,1,5,4,3,0:T(8,128)(2,1)} %copy.40) | data formatting | bytes 3538944 | tf_op jit(solution)/shard_map/reshape.120
  273.3 2.4 copy.52
  277.8 2.8 fusion.100
  280.6 2.4 copy.41
  282.9 2.1 fusion.101
  285.1 2.7 broadcast_select_fusion.14
  287.8 2.5 fusion.110
  290.3 3.7 broadcast_select_fusion.54
  301.9 8.0 %copy.42 = bf16[1,27,64,2,16,16]{2,1,5,4,3,0:T(8,128)(2,1)} copy(bf16[1,27,64,2,16,16]{2,5,4,3,1,0:T(8,128)(2,1)} %constant_dynamic-update-slice_fusion.189) | data formatting | bytes 3538944 | tf_op jit(solution)/shard_map/stack | solution.py:54
  309.9 6.8 %reshape.1531 = bf16[1728,512]{0,1:T(8,128)(2,1)} reshape(bf16[1,27,64,2,16,16]{2,1,5,4,3,0:T(8,128)(2,1)} %copy.42) | data formatting | bytes 3538944 | tf_op jit(solution)/shard_map/reshape.122
  316.7 2.1 convolution_add_fusion.6
  328.5 2.3 fusion.15
  330.8 2.3 fusion.14
  368.7 6.0 %copy.45 = bf16[1,27,64,2,16,16]{2,1,5,4,3,0:T(8,128)(2,1)} copy(bf16[1,27,64,2,16,16]{2,5,4,3,1,0:T(8,128)(2,1)S(1)} %constant_dynamic-update-slice_fusion.216) | data formatting | bytes 3538944 | tf_op jit(solution)/shard_map/stack | solution.py:54
  374.7 6.4 %reshape.1532 = bf16[1728,512]{0,1:T(8,128)(2,1)} reshape(bf16[1,27,64,2,16,16]{2,1,5,4,3,0:T(8,128)(2,1)} %copy.45) | data formatting | bytes 3538944 | tf_op jit(solution)/shard_map/reshape.180
  381.0 8.0 %copy.46 = bf16[1,27,64,2,16,16]{2,1,5,4,3,0:T(8,128)(2,1)} copy(bf16[1,27,64,2,16,16]{2,5,4,3,1,0:T(8,128)(2,1)} %get-tuple-element.19) | data formatting | bytes 3538944 | tf_op jit(solution)/shard_map/stack | solution.py:54
  389.0 6.5 %reshape.1534 = bf16[1728,512]{0,1:T(8,128)(2,1)} reshape(bf16[1,27,64,2,16,16]{2,1,5,4,3,0:T(8,128)(2,1)} %copy.46) | data formatting | bytes 3538944 | tf_op jit(solution)/shard_map/reshape.182
  395.6 8.0 %copy.47 = bf16[1,27,64,2,16,16]{2,1,5,4,3,0:T(8,128)(2,1)} copy(bf16[1,27,64,2,16,16]{2,5,4,3,1,0:T(8,128)(2,1)} %get-tuple-element.18) | data formatting | bytes 3538944 | tf_op jit(solution)/shard_map/stack | solution.py:54
  403.6 6.3 %reshape.1535 = bf16[1728,512]{0,1:T(8,128)(2,1)} reshape(bf16[1,27,64,2,16,16]{2,1,5,4,3,0:T(8,128)(2,1)} %copy.47) | data formatting | bytes 3538944 | tf_op jit(solution)/shard_map/reshape.184
  409.9 8.0 %copy.48 = bf16[1,27,64,2,16,16]{2,1,5,4,3,0:T(8,128)(2,1)} copy(bf16[1,27,64,2,16,16]{2,5,4,3,1,0:T(8,128)(2,1)} %get-tuple-element.17) | data formatting | bytes 3538944 | tf_op jit(solution)/shard_map/stack | solution.py:54
  417.9 6.8 %reshape.1536 = bf16[1728,512]{0,1:T(8,128)(2,1)} reshape(bf16[1,27,64,2,16,16]{2,1,5,4,3,0:T(8,128)(2,1)} %copy.48) | data formatting | bytes 3538944 | tf_op jit(solution)/shard_map/reshape.186
  424.7 8.0 %copy.49 = bf16[1,27,64,2,16,16]{2,1,5,4,3,0:T(8,128)(2,1)} copy(bf16[1,27,64,2,16,16]{2,5,4,3,1,0:T(8,128)(2,1)} %get-tuple-element.16) | data formatting | bytes 3538944 | tf_op jit(solution)/shard_map/stack | solution.py:54
  432.7 6.4 %reshape.1537 = bf16[1728,512]{0,1:T(8,128)(2,1)} reshape(bf16[1,27,64,2,16,16]{2,1,5,4,3,0:T(8,128)(2,1)} %copy.49) | data formatting | bytes 3538944 | tf_op jit(solution)/shard_map/reshape.188
  439.0 8.0 %copy.50 = bf16[1,27,64,2,16,16]{2,1,5,4,3,0:T(8,128)(2,1)} copy(bf16[1,27,64,2,16,16]{2,5,4,3,1,0:T(8,128)(2,1)} %get-tuple-element.15) | data formatting | bytes 3538944 | tf_op jit(solution)/shard_map/stack | solution.py:54
  447.0 6.5 %reshape.1538 = bf16[1728,512]{0,1:T(8,128)(2,1)} reshape(bf16[1,27,64,2,16,16]{2,1,5,4,3,0:T(8,128)(2,1)} %copy.50) | data formatting | bytes 3538944 | tf_op jit(solution)/shard_map/reshape.190
  453.5 8.0 %copy.51 = bf16[1,27,64,2,16,16]{2,1,5,4,3,0:T(8,128)(2,1)} copy(bf16[1,27,64,2,16,16]{2,5,4,3,1,0:T(8,128)(2,1)} %get-tuple-element.14) | data formatting | bytes 3538944 | tf_op jit(solution)/shard_map/stack | solution.py:54
  461.5 6.4 %reshape.1539 = bf16[1728,512]{0,1:T(8,128)(2,1)} reshape(bf16[1,27,64,2,16,16]{2,1,5,4,3,0:T(8,128)(2,1)} %copy.51) | data formatting | bytes 3538944 | tf_op jit(solution)/shard_map/reshape.192
  467.9 8.0 %copy.53 = bf16[1,27,64,2,16,16]{2,1,5,4,3,0:T(8,128)(2,1)} copy(bf16[1,27,64,2,16,16]{2,5,4,3,1,0:T(8,128)(2,1)} %copy-done.27) | data formatting | bytes 3538944 | tf_op jit(solution)/shard_map/stack | solution.py:54
  475.9 6.6 %reshape.1540 = bf16[1728,512]{0,1:T(8,128)(2,1)} reshape(bf16[1,27,64,2,16,16]{2,1,5,4,3,0:T(8,128)(2,1)} %copy.53) | data formatting | bytes 3538944 | tf_op jit(solution)/shard_map/reshape.194
  482.5 2.3 fusion.7
  484.8 2.3 fusion.6
  492.5 95.4 %all-reduce.2.cloned.1.call-done = f32[27,64,64]{2,0,1:T(8,128)} async-done(((f32[27,64,64]{2,0,1:T(8,128)}), f32[27,64,64]{2,0,1:T(8,128)}) %all-reduce.2.cloned.1.call-update) | async-done | bytes 442384 | tf_op jit(solution)/shard_map/psum | solution.py:112
  587.8 2.7 copy.54
  (297 shorter events, 120.9 us)
Async XLA Ops:
  7.2 22.3 %copy-start.53 = (bf16[1,1,64,4096]{3,2,1,0:T(8,128)(2,1)S(1)}, bf16[1,1,64,4096]{3,2,1,0:T(8,128)(2,1)}, u32[]{:S(2)}) copy-start(bf16[1,1,64,4096]{3,2,1,0:T(8,128)(2,1)} %param.5) | copy-start | bytes 1572868
  7.2 580.6 %all-reduce.2.cloned.1.call-start = ((), (), s32[]{:S(2)}) async-start(), calls=%async_computation | async-start | bytes 2097152 | tf_op jit(solution)/shard_map/psum | solution.py:112
  10.3 103.6 %collective-permute-start = (bf16[1,64,4096]{2,1,0:T(8,128)(2,1)}, bf16[1,64,4096]{2,1,0:T(8,128)(2,1)}, u32[]{:S(2)}, u32[]{:S(2)}) collective-permute-start(bf16[1,64,4096]{2,1,0:T(8,128)(2,1)} %get-tuple-element.466), channel_id=1, source_target_pairs={{0,1},{1,2},{2,3},{3,4},{4,5},{5,6},{6,7},{7,8},{8,9},{9,10},{10,1... | collective-permute-start | bytes 1572872 | tf_op jit(solution)/shard_map/ppermute | solution.py:17
  15.1 265.5 %collective-permute-start.1 = (bf16[1,64,4096]{2,1,0:T(8,128)(2,1)}, bf16[1,64,4096]{2,1,0:T(8,128)(2,1)}, u32[]{:S(2)}, u32[]{:S(2)}) collective-permute-start(bf16[1,64,4096]{2,1,0:T(8,128)(2,1)} %get-tuple-element.466), channel_id=1, source_target_pairs={{1,0},{2,1},{3,2},{4,3},{5,4},{6,5},{7,6},{8,7},{9,8},{10,9},{11,1... | collective-permute-start | bytes 1572872 | tf_op jit(solution)/shard_map/ppermute | solution.py:18
  16.4 256.9 %collective-permute-start.3 = (bf16[1,64,4096]{2,1,0:T(8,128)(2,1)}, bf16[1,64,4096]{2,1,0:T(8,128)(2,1)}, u32[]{:S(2)}, u32[]{:S(2)}) collective-permute-start(bf16[1,64,4096]{2,1,0:T(8,128)(2,1)} %get-tuple-element.465), channel_id=1, source_target_pairs={{1,0},{2,1},{3,2},{4,3},{5,4},{6,5},{7,6},{8,7},{9,8},{10,9},{11,1... | collective-permute-start | bytes 1572872 | tf_op jit(solution)/shard_map/ppermute | solution.py:18
  17.7 115.5 %collective-permute-start.2 = (bf16[1,64,4096]{2,1,0:T(8,128)(2,1)}, bf16[1,64,4096]{2,1,0:T(8,128)(2,1)}, u32[]{:S(2)}, u32[]{:S(2)}) collective-permute-start(bf16[1,64,4096]{2,1,0:T(8,128)(2,1)} %get-tuple-element.465), channel_id=1, source_target_pairs={{0,1},{1,2},{2,3},{3,4},{4,5},{5,6},{6,7},{7,8},{8,9},{9,10},{10,1... | collective-permute-start | bytes 1572872 | tf_op jit(solution)/shard_map/ppermute | solution.py:17
  27.0 37.8 %copy-start.63 = (pred[1,27]{1,0:T(4,128)(4,1)}, pred[1,27]{1,0:T(4,128)(4,1)S(1)}, u32[]{:S(2)}) copy-start(pred[1,27]{1,0:T(4,128)(4,1)S(1)} %bitcast_compare_fusion) | copy-start | bytes 85
  73.2 28.0 %copy-start.33 = (bf16[1,64,16,1,1]{1,4,3,2,0:T(2,128)(2,1)}, bf16[1,64,16,1,1]{1,4,3,2,0:T(2,128)(2,1)S(1)}, u32[]{:S(2)}) copy-start(bf16[1,64,16,1,1]{1,4,3,2,0:T(2,128)(2,1)S(1)} %get-tuple-element.407) | copy-start | bytes 6148
  73.2 28.0 %copy-start.35 = (bf16[1,64,16,1,1]{1,4,3,2,0:T(2,128)(2,1)}, bf16[1,64,16,1,1]{1,4,3,2,0:T(2,128)(2,1)S(1)}, u32[]{:S(2)}) copy-start(bf16[1,64,16,1,1]{1,4,3,2,0:T(2,128)(2,1)S(1)} %get-tuple-element.408) | copy-start | bytes 6148
  73.2 28.0 %copy-start.37 = (bf16[1,64,16,1,1]{1,4,3,2,0:T(2,128)(2,1)}, bf16[1,64,16,1,1]{1,4,3,2,0:T(2,128)(2,1)S(1)}, u32[]{:S(2)}) copy-start(bf16[1,64,16,1,1]{1,4,3,2,0:T(2,128)(2,1)S(1)} %get-tuple-element.409) | copy-start | bytes 6148
  73.2 28.0 %copy-start.39 = (bf16[1,64,16,1,1]{1,4,3,2,0:T(2,128)(2,1)}, bf16[1,64,16,1,1]{1,4,3,2,0:T(2,128)(2,1)S(1)}, u32[]{:S(2)}) copy-start(bf16[1,64,16,1,1]{1,4,3,2,0:T(2,128)(2,1)S(1)} %get-tuple-element.410) | copy-start | bytes 6148
  76.2 24.9 %copy-start.5 = (bf16[27,64,64]{2,1,0:T(8,128)(2,1)S(1)}, bf16[27,64,64]{2,1,0:T(8,128)(2,1)}, u32[]{:S(2)}) copy-start(bf16[27,64,64]{2,1,0:T(8,128)(2,1)} %param.7) | copy-start | bytes 663556
  103.7 5.9 copy-start.64
  103.7 6.6 %copy-start.41 = (bf16[1,64,16,1,1]{1,4,3,2,0:T(2,128)(2,1)S(1)}, bf16[1,64,16,1,1]{1,4,3,2,0:T(2,128)(2,1)}, u32[]{:S(2)}) copy-start(bf16[1,64,16,1,1]{1,4,3,2,0:T(2,128)(2,1)} %get-tuple-element.453) | copy-start | bytes 6148
  103.7 6.6 %copy-start.44 = (bf16[1,64,16,1,1]{1,4,3,2,0:T(2,128)(2,1)S(1)}, bf16[1,64,16,1,1]{1,4,3,2,0:T(2,128)(2,1)}, u32[]{:S(2)}) copy-start(bf16[1,64,16,1,1]{1,4,3,2,0:T(2,128)(2,1)} %get-tuple-element.454) | copy-start | bytes 6148
  103.7 6.6 %copy-start.47 = (bf16[1,64,16,1,1]{1,4,3,2,0:T(2,128)(2,1)S(1)}, bf16[1,64,16,1,1]{1,4,3,2,0:T(2,128)(2,1)}, u32[]{:S(2)}) copy-start(bf16[1,64,16,1,1]{1,4,3,2,0:T(2,128)(2,1)} %get-tuple-element.455) | copy-start | bytes 6148
  103.8 6.6 %copy-start.50 = (bf16[1,64,16,1,1]{1,4,3,2,0:T(2,128)(2,1)S(1)}, bf16[1,64,16,1,1]{1,4,3,2,0:T(2,128)(2,1)}, u32[]{:S(2)}) copy-start(bf16[1,64,16,1,1]{1,4,3,2,0:T(2,128)(2,1)} %get-tuple-element.456) | copy-start | bytes 6148
  116.2 11.8 %copy-start.42 = (bf16[1,64,16,1,1]{1,4,3,2,0:T(2,128)(2,1)S(1)}, bf16[1,64,16,1,1]{1,4,3,2,0:T(2,128)(2,1)}, u32[]{:S(2)}) copy-start(bf16[1,64,16,1,1]{1,4,3,2,0:T(2,128)(2,1)} %get-tuple-element.453) | copy-start | bytes 6148
  116.2 11.8 %copy-start.45 = (bf16[1,64,16,1,1]{1,4,3,2,0:T(2,128)(2,1)S(1)}, bf16[1,64,16,1,1]{1,4,3,2,0:T(2,128)(2,1)}, u32[]{:S(2)}) copy-start(bf16[1,64,16,1,1]{1,4,3,2,0:T(2,128)(2,1)} %get-tuple-element.454) | copy-start | bytes 6148
  116.2 11.8 %copy-start.48 = (bf16[1,64,16,1,1]{1,4,3,2,0:T(2,128)(2,1)S(1)}, bf16[1,64,16,1,1]{1,4,3,2,0:T(2,128)(2,1)}, u32[]{:S(2)}) copy-start(bf16[1,64,16,1,1]{1,4,3,2,0:T(2,128)(2,1)} %get-tuple-element.455) | copy-start | bytes 6148
  116.2 11.8 %copy-start.51 = (bf16[1,64,16,1,1]{1,4,3,2,0:T(2,128)(2,1)S(1)}, bf16[1,64,16,1,1]{1,4,3,2,0:T(2,128)(2,1)}, u32[]{:S(2)}) copy-start(bf16[1,64,16,1,1]{1,4,3,2,0:T(2,128)(2,1)} %get-tuple-element.456) | copy-start | bytes 6148
  135.7 10.5 %copy-start.3 = (bf16[1,64,16,17,18]{1,4,3,2,0:T(8,128)(2,1)S(1)}, bf16[1,64,16,17,18]{1,4,3,2,0:T(8,128)(2,1)}, u32[]{:S(2)}) copy-start(bf16[1,64,16,17,18]{1,4,3,2,0:T(8,128)(2,1)} %get-tuple-element.279) | copy-start | bytes 1880068
  135.7 12.7 %copy-start.4 = (bf16[1,64,16,17,18]{1,4,3,2,0:T(8,128)(2,1)S(1)}, bf16[1,64,16,17,18]{1,4,3,2,0:T(8,128)(2,1)}, u32[]{:S(2)}) copy-start(bf16[1,64,16,17,18]{1,4,3,2,0:T(8,128)(2,1)} %get-tuple-element.280) | copy-start | bytes 1880068
  168.9 4.6 copy-start.29
  168.9 4.6 copy-start.30
  168.9 4.6 copy-start.31
  168.9 5.0 copy-start.32
  282.9 13.8 %copy-start.43 = (bf16[1,64,16,1,1]{1,4,3,2,0:T(2,128)(2,1)S(1)}, bf16[1,64,16,1,1]{1,4,3,2,0:T(2,128)(2,1)}, u32[]{:S(2)}) copy-start(bf16[1,64,16,1,1]{1,4,3,2,0:T(2,128)(2,1)} %get-tuple-element.453) | copy-start | bytes 6148
  282.9 13.8 %copy-start.46 = (bf16[1,64,16,1,1]{1,4,3,2,0:T(2,128)(2,1)S(1)}, bf16[1,64,16,1,1]{1,4,3,2,0:T(2,128)(2,1)}, u32[]{:S(2)}) copy-start(bf16[1,64,16,1,1]{1,4,3,2,0:T(2,128)(2,1)} %get-tuple-element.454) | copy-start | bytes 6148
  282.9 13.8 %copy-start.49 = (bf16[1,64,16,1,1]{1,4,3,2,0:T(2,128)(2,1)S(1)}, bf16[1,64,16,1,1]{1,4,3,2,0:T(2,128)(2,1)}, u32[]{:S(2)}) copy-start(bf16[1,64,16,1,1]{1,4,3,2,0:T(2,128)(2,1)} %get-tuple-element.455) | copy-start | bytes 6148
  282.9 13.8 %copy-start.52 = (bf16[1,64,16,1,1]{1,4,3,2,0:T(2,128)(2,1)S(1)}, bf16[1,64,16,1,1]{1,4,3,2,0:T(2,128)(2,1)}, u32[]{:S(2)}) copy-start(bf16[1,64,16,1,1]{1,4,3,2,0:T(2,128)(2,1)} %get-tuple-element.456) | copy-start | bytes 6148
  309.9 6.8 %copy-start.54 = (f32[64,1728]{1,0:T(8,128)S(1)}, f32[64,1728]{1,0:T(8,128)}, u32[]{:S(2)}) copy-start(f32[64,1728]{1,0:T(8,128)} %fusion.100) | copy-start | bytes 1327108
  316.7 2.2 copy-start.6
  316.7 3.6 copy-start.8
  316.7 5.0 copy-start.10
  318.9 4.3 copy-start.12
  320.3 4.2 copy-start.14
  321.7 4.0 copy-start.16
  328.5 4.6 copy-start.7
  328.5 5.3 copy-start.9
  330.8 3.7 copy-start.11
  333.8 2.2 copy-start.15
  334.5 2.2 copy-start.17
  335.2 2.2 copy-start.25
  335.2 2.2 copy-start.34
  335.2 2.2 copy-start.36
  335.3 2.2 copy-start.38
  335.3 2.2 copy-start.40
  335.3 2.2 copy-start.57
  335.3 2.2 copy-start.58
  335.3 2.2 copy-start.61
  338.4 4.4 copy-start.2
  362.8 3.7 copy-start.24
  362.8 3.7 copy-start.55
  362.8 3.7 copy-start.56
  362.8 3.7 copy-start.59
  362.8 3.7 copy-start.60
  362.8 3.7 copy-start.66
  362.8 3.7 copy-start.67
  362.8 3.7 copy-start.68
  362.8 3.7 copy-start.69
  482.5 4.7 copy-start.18
  482.5 5.4 copy-start.19
  484.8 3.7 copy-start.20
  (15 other events, 29.5 us)
Sparse Core Ops, SparseCore 0:
  328.6 259.1 all-reduce.1
where the time goes:
time: 609 us; the launch traced here: 598 us
  local copies, waits for them, and re-layouts  300 us (49%)
  waiting for transfers between devices  95.4 us (16%)
  other arithmetic  93.2 us (15%)
  between operations  66.2 us (11%)
  matrix products  30.4 us (5%)
  starting transfers between devices  12.9 us (2%)
    another operation x18, local copies, waits for them, and re-layouts, stacked_block(): joined = jnp.stack(pieces, axis=1)  125 us
    another operation x16, local copies, waits for them, and re-layouts  104 us
    psum x1, waiting for transfers between devices, local(): grad_weight = lax.psum(partial_weight, ('scan', 'brick'))  95.4 us
    unnamed x197, local copies, waits for them, and re-layouts  53.8 us
    select_n x19, other arithmetic, assemble(): jnp.where(valid_rows[:, k][:, None, None, None, None], fetched, jnp.zeros...  46.4 us
    unnamed x54, other arithmetic  33.3 us
    dot_general x8, matrix products, local(): jnp.einsum('bov,bmv->om', up_block, forward_stack, preferred_element_type...  13 us
  transfers between devices with their start and end apart: 5, of which 1 were waited for; matrix products, arithmetic and copies ran while one was open for 61% of the time, Pallas kernels for 0%

commit v1 on v0

v1 whole, which is shorter than its diff:
```python
import jax
import jax.numpy as jnp
from jax import lax
from jax.experimental import pallas as pl
from jax.experimental.pallas import tpu as pltpu
from jax.sharding import PartitionSpec as P

C = 64
BS = 16
PLANE = BS * BS
V = BS * PLANE
EXT = (BS + 2) * PLANE
TAPS = 9
BF = jnp.bfloat16
F32 = jnp.float32
MESH = pl.DeviceIdType.MESH
N_CORE, N_X, N_Y, N_Z = 2, 4, 4, 8
N_BRICK = N_Y * N_Z
N_XY = N_X * N_Y


def spread(plane, x_iota):
    left = jnp.where(x_iota == 0, pltpu.roll(plane, PLANE - 15, 1), pltpu.roll(plane, 1, 1))
    right = jnp.where(x_iota == BS - 1, pltpu.roll(plane, 15, 1), pltpu.roll(plane, PLANE - 1, 1))
    shifted = []
    for dy in (-1, 0, 1):
        for base in (left, plane, right):
            shifted.append(base if dy == 0 else pltpu.roll(base, (-dy * BS) % PLANE, 1))
    return shifted


def kernel(
    feat_hbm, cot_hbm, w_ref, nb_ref, occ_ref,
    out_hbm, gin_hbm, gw_ref,
    feat_v, cot_v, out_v, gin_v, mask_v, s9f, s9u, u3, wf, wb,
    halo_send, halo_recv, part, pair_recv, half, xy_recv, own, z_recv, total, final,
    in_sem, out_sem, halo_ssem, halo_rsem, ar_ssem, ar_rsem,
):
    scan = lax.axis_index("scan")
    brick = lax.axis_index("brick")
    cx, cc = scan // N_CORE, scan % N_CORE
    cz, cy = brick // N_Y, brick % N_Y
    xy = cx * N_Y + cy
    up_dev = (scan, lax.rem(brick + 1, N_BRICK))
    down_dev = (scan, lax.rem(brick + N_BRICK - 1, N_BRICK))
    pair_dev = (cx * N_CORE + 1 - cc, brick)

    def xy_peer(j):
        i = lax.rem(xy + j, N_XY)
        return i, ((i // N_Y) * N_CORE + cc, cz * N_Y + lax.rem(i, N_Y))

    def z_peer(j):
        return (scan, lax.rem(cz + j, N_Z) * N_Y + cy)

    feat_in = pltpu.make_async_copy(feat_hbm, feat_v, in_sem.at[0])
    cot_in = pltpu.make_async_copy(cot_hbm, cot_v, in_sem.at[1])
    feat_in.start()
    cot_in.start()

    barrier = pltpu.get_barrier_semaphore()
    signals = 0
    for dev in [up_dev, down_dev, pair_dev]:
        pl.semaphore_signal(barrier, inc=1, device_id=dev, device_id_type=MESH)
        signals += 1
    for j in range(1, N_XY):
        pl.semaphore_signal(barrier, inc=1, device_id=xy_peer(j)[1], device_id_type=MESH)
        signals += 1
    for j in range(1, N_Z):
        pl.semaphore_signal(barrier, inc=1, device_id=z_peer(j), device_id_type=MESH)
        signals += 1

    lane = lax.broadcasted_iota(jnp.int32, (C, PLANE), 1)
    x_iota = lane % BS
    y_iota = lane // BS
    for layer in range(3):
        flag = [jnp.where(nb_ref[0, 9 * layer + k] >= 0, 1.0, 0.0).astype(F32) for k in range(9)]
        for dy in (-1, 0, 1):
            y_out = y_iota == (BS - 1 if dy == 1 else 0 if dy == -1 else -1)
            for dx in (-1, 0, 1):
                x_out = x_iota == (BS - 1 if dx == 1 else 0 if dx == -1 else -1)

                def at(a, b):
                    return flag[3 * (a + 1) + b + 1]

                inner = jnp.where(x_out, at(0, dx), at(0, 0))
                outer = jnp.where(x_out, at(dy, dx), at(dy, 0))
                mask_v[layer, 3 * (dy + 1) + dx + 1] = jnp.where(y_out, outer, inner).astype(BF)

    def occ_at(z):
        return occ_ref[:, pl.ds(z * PLANE, PLANE)].astype(F32)

    feat_in.wait()
    for n, z in enumerate((BS - 1, 0)):
        halo_send[0, n] = (feat_v[:, z * PLANE : (z + 1) * PLANE].astype(F32) * occ_at(z)).astype(BF)
    pl.semaphore_wait(barrier, signals)

    def halo_copy(field, n):
        return pltpu.make_async_remote_copy(
            src_ref=halo_send.at[field, n],
            dst_ref=halo_recv.at[field, n],
            send_sem=halo_ssem.at[field, n],
            recv_sem=halo_rsem.at[field, n],
            device_id=(up_dev, down_dev)[n],
            device_id_type=MESH,
        )

    halos = [[halo_copy(field, n) for n in range(2)] for field in range(2)]
    halos[0][0].start()
    halos[0][1].start()

    def fill(s9, plane, layer, slot):
        lanes = pl.ds(pl.multiple_of(slot * PLANE, PLANE), PLANE)
        for k, moved in enumerate(spread(plane, x_iota)):
            s9[k * C : (k + 1) * C, lanes] = moved.astype(BF) * mask_v[layer, k]

    cot_in.wait()
    for n, z in enumerate((BS - 1, 0)):
        halo_send[1, n] = (cot_v[:, z * PLANE : (z + 1) * PLANE].astype(F32) * occ_at(z)).astype(BF)
    halos[1][0].start()
    halos[1][1].start()

    u3[...] = jnp.zeros_like(u3)

    def own_planes(z, carry):
        z0 = pl.multiple_of(z * PLANE, PLANE)
        occ = occ_ref[:, pl.ds(z0, PLANE)].astype(F32)
        live = feat_v[:, pl.ds(z0, PLANE)].astype(F32) * occ
        fill(s9f, live, 1, z + 1)
        ups = (cot_v[:, pl.ds(z0, PLANE)].astype(F32) * occ).astype(BF)
        for dz in range(3):
            u3[dz * C : (dz + 1) * C, pl.ds(pl.multiple_of((z + dz) * PLANE, PLANE), PLANE)] = ups
        return carry

    lax.fori_loop(0, BS, own_planes, 0)

    halos[0][0].wait_recv()
    halos[0][1].wait_recv()
    fill(s9f, halo_recv[0, 0].astype(F32), 0, 0)
    fill(s9f, halo_recv[0, 1].astype(F32), 2, BS + 1)

    for t in range(3):
        width = min(PLANE, TAPS * C - t * PLANE)
        g = lax.dot_general(
            u3[...], s9f[t * PLANE : t * PLANE + width, :],
            (((1,), (1,)), ((), ())), preferred_element_type=F32,
        )
        for n in range(0, width, 128):
            for r in range(6):
                w = min(128, width - n)
                part[(2 * t + n // 128) * 6 + r, :, 0:w] = g[32 * r : 32 * r + 32, n : n + w]
    part[24:30, :, C:128] = jnp.zeros((6, 32, C), F32)
    part[30:32] = jnp.zeros((2, 32, 128), F32)

    pair = pltpu.make_async_remote_copy(
        src_ref=part.at[pl.ds((1 - cc) * N_XY, N_XY)],
        dst_ref=pair_recv,
        send_sem=ar_ssem.at[0],
        recv_sem=ar_rsem.at[0],
        device_id=pair_dev,
        device_id_type=MESH,
    )
    pair.start()

    for k in range(27):
        dz, j = k // 9, k % 9
        wf[dz * C : (dz + 1) * C, j * C : (j + 1) * C] = w_ref[k]
        wb[dz * C : (dz + 1) * C, j * C : (j + 1) * C] = jnp.transpose(w_ref[26 - k].astype(F32)).astype(BF)

    pair.wait_recv()
    half[...] = part[pl.ds(cc * N_XY, N_XY)] + pair_recv[...]

    def xy_copy(j):
        i, dev = xy_peer(j)
        return pltpu.make_async_remote_copy(
            src_ref=half.at[i],
            dst_ref=xy_recv.at[j],
            send_sem=ar_ssem.at[j],
            recv_sem=ar_rsem.at[j],
            device_id=dev,
            device_id_type=MESH,
        )

    xy_order = [10, 9, 11, 6, 7, 5, 14, 8, 2, 13, 3, 1, 15, 4, 12]
    xy_copies = {j: xy_copy(j) for j in xy_order}
    for j in xy_order:
        xy_copies[j].start()

    def convolve(weights, s9, dst):
        def product(slot):
            return jnp.dot(
                weights[...], s9[:, pl.ds(pl.multiple_of(slot * PLANE, PLANE), PLANE)],
                preferred_element_type=F32,
            )

        first = product(0)
        second = product(1)

        def step(z, carry):
            low, mid = carry
            r = product(z + 2)
            z0 = pl.multiple_of(z * PLANE, PLANE)
            occ = occ_ref[:, pl.ds(z0, PLANE)].astype(F32)
            dst[:, pl.ds(z0, PLANE)] = ((mid + r[2 * C :]) * occ).astype(BF)
            return r[:C], low + r[C : 2 * C]

        lax.fori_loop(0, BS, step, (second[:C], first[:C] + second[C : 2 * C]))

    convolve(wf, s9f, out_v)
    out_copy = pltpu.make_async_copy(out_v, out_hbm, out_sem.at[0])
    out_copy.start()

    for j in xy_order:
        xy_copies[j].wait_recv()
    own[...] = half[xy]
    for j in range(1, N_XY):
        own[...] += xy_recv[j]

    def z_copy(j):
        return pltpu.make_async_remote_copy(
            src_ref=own,
            dst_ref=z_recv.at[j],
            send_sem=ar_ssem.at[16 + j],
            recv_sem=ar_rsem.at[16 + j],
            device_id=z_peer(j),
            device_id_type=MESH,
        )

    z_order = [4, 3, 5, 2, 6, 1, 7]
    z_copies = {j: z_copy(j) for j in z_order}
    for j in z_order:
        z_copies[j].start()

    halos[1][0].wait_recv()
    halos[1][1].wait_recv()
    fill(s9u, halo_recv[1, 0].astype(F32), 0, 0)
    fill(s9u, halo_recv[1, 1].astype(F32), 2, BS + 1)

    def up_planes(z, carry):
        z0 = pl.multiple_of((z + 1) * PLANE, PLANE)
        fill(s9u, u3[C : 2 * C, pl.ds(z0, PLANE)].astype(F32), 1, z + 1)
        return carry

    lax.fori_loop(0, BS, up_planes, 0)
    convolve(wb, s9u, gin_v)
    gin_copy = pltpu.make_async_copy(gin_v, gin_hbm, out_sem.at[1])
    gin_copy.start()

    for j in z_order:
        z_copies[j].wait_recv()
    z_recv[0] = own[...]
    total[...] = z_recv[cz]
    for s in range(1, N_Z):
        total[...] += z_recv[lax.rem(cz + N_Z - s, N_Z)]

    def back_copy(j):
        i, dev = xy_peer(j)
        return pltpu.make_async_remote_copy(
            src_ref=total,
            dst_ref=final.at[cc * N_XY + xy],
            send_sem=ar_ssem.at[24 + j],
            recv_sem=ar_rsem.at[24 + j],
            device_id=dev,
            device_id_type=MESH,
        )

    back_copies = {j: back_copy(j) for j in xy_order}
    for j in xy_order:
        back_copies[j].start()
    final[cc * N_XY + xy] = total[...]
    for j in xy_order:
        back_copies[j].wait_recv()
    last = pltpu.make_async_remote_copy(
        src_ref=final.at[pl.ds(cc * N_XY, N_XY)],
        dst_ref=final.at[pl.ds(cc * N_XY, N_XY)],
        send_sem=ar_ssem.at[40],
        recv_sem=ar_rsem.at[40],
        device_id=pair_dev,
        device_id_type=MESH,
    )
    last.start()
    last.wait_recv()
    for k in range(27):
        dz, j = k // 9, k % 9
        for h in range(2):
            gw_ref[k, 32 * h : 32 * h + 32, :] = final[(j // 2) * 6 + 2 * dz + h, :, (j % 2) * C : (j % 2 + 1) * C]

    pair.wait_send()
    last.wait_send()
    for j in xy_order:
        xy_copies[j].wait_send()
        back_copies[j].wait_send()
    for j in z_order:
        z_copies[j].wait_send()
    for field in range(2):
        for n in range(2):
            halos[field][n].wait_send()
    out_copy.wait()
    gin_copy.wait()


def local(features, cotangent, weight, neighbours, occupancy):
    vmem = pl.BlockSpec(memory_space=pltpu.VMEM)
    anywhere = pl.BlockSpec(memory_space=pl.ANY)
    field = jax.ShapeDtypeStruct((C, V), BF)
    output, grad_input, grad_weight = pl.pallas_call(
        kernel,
        out_shape=(field, field, jax.ShapeDtypeStruct((27, C, C), F32)),
        in_specs=[anywhere, anywhere, vmem, pl.BlockSpec(memory_space=pltpu.SMEM), vmem],
        out_specs=(anywhere, anywhere, vmem),
        scratch_shapes=[
            pltpu.VMEM((C, V), BF),
            pltpu.VMEM((C, V), BF),
            pltpu.VMEM((C, V), BF),
            pltpu.VMEM((C, V), BF),
            pltpu.VMEM((3, TAPS, C, PLANE), BF),
            pltpu.VMEM((TAPS * C, EXT), BF),
            pltpu.VMEM((TAPS * C, EXT), BF),
            pltpu.VMEM((3 * C, EXT), BF),
            pltpu.VMEM((3 * C, TAPS * C), BF),
            pltpu.VMEM((3 * C, TAPS * C), BF),
            pltpu.VMEM((2, 2, C, PLANE), BF),
            pltpu.VMEM((2, 2, C, PLANE), BF),
            pltpu.VMEM((32, 32, 128), F32),
            pltpu.VMEM((16, 32, 128), F32),
            pltpu.VMEM((16, 32, 128), F32),
            pltpu.VMEM((16, 32, 128), F32),
            pltpu.VMEM((32, 128), F32),
            pltpu.VMEM((8, 32, 128), F32),
            pltpu.VMEM((32, 128), F32),
            pltpu.VMEM((32, 32, 128), F32),
            pltpu.SemaphoreType.DMA((2,)),
            pltpu.SemaphoreType.DMA((2,)),
            pltpu.SemaphoreType.DMA((2, 2)),
            pltpu.SemaphoreType.DMA((2, 2)),
            pltpu.SemaphoreType.DMA((41,)),
            pltpu.SemaphoreType.DMA((41,)),
        ],
        compiler_params=pltpu.CompilerParams(
            collective_id=0, has_side_effects=True, vmem_limit_bytes=50 * 2**20
        ),
    )(
        features.reshape(C, V), cotangent.reshape(C, V), weight,
        neighbours.reshape(1, 27), occupancy.reshape(1, V),
    )
    return output.reshape(1, 1, C, V), grad_input.reshape(1, 1, C, V), grad_weight


def solution(mesh):
    in_specs = (
        P("scan", "brick", None, None),
        P("scan", "brick", None, None),
        P(),
        P("scan", "brick", None),
        P("scan", "brick", None),
    )
    out_specs = (P("scan", "brick", None, None), P("scan", "brick", None, None), P())
    return jax.shard_map(local, mesh=mesh, in_specs=in_specs, out_specs=out_specs, check_vma=False)
```

time: 609 us -> 49.1 us (0.08); the launches traced: 598 us -> 48.8 us
  local copies, waits for them, and re-layouts: 300 us -> 6.96 us
  waiting for transfers between devices: 95.4 us -> 0 us
  other arithmetic: 93.2 us -> 0 us
  between operations: 66.2 us -> 0.65 us
  Pallas kernels: 0 us -> 41.2 us
  matrix products: 30.4 us -> 0 us
  starting transfers between devices: 12.9 us -> 0 us
    another operation x34 -> x0, local copies, waits for them, and re-layouts: 229 us -> none  [the longest x18 125 us: stacked_block(): joined = jnp.stack(pieces, axis=1)]
    psum x1 -> x0, waiting for transfers between devices: 95.4 us -> none  [local(): grad_weight = lax.psum(partial_weight, ('scan', 'brick'))]
    select_n x20 -> x0, other arithmetic: 47.1 us -> none  [the longest x19 46.4 us: assemble(): jnp.where(valid_rows[:, k][:, None, None, None, None], fetched, jnp.zeros...]
    unnamed x197 -> x13, local copies, waits for them, and re-layouts: 53.8 us -> 6.96 us
    pallas_call x0 -> x1, Pallas kernels: none -> 41.2 us  [local(): pl.pallas_call(kernel, out_shape=(field, field, jax.ShapeDtypeStruct((27,...]
    unnamed x54 -> x0, other arithmetic: 33.3 us -> none
    dot_general x24 -> x0, matrix products: 30.4 us -> none  [the longest x8 13 us: local(): jnp.einsum('bov,bmv->om', up_block, forward_stack, preferred_element_type...]
    ppermute x4 -> x0, starting transfers between devices: 12.9 us -> none  [the longest x2 10.3 us: with_halo(): before = lax.ppermute(last, axis, up)]
  transfers between devices with their start and end apart: 5 -> 0, of which waited for: 1 -> 0; matrix products, arithmetic and copies ran while one was open for 61% -> 0% of each run, Pallas kernels for 0% -> 0%
where the time goes in v1:
time: 49.1 us; the launch traced here: 48.8 us
  Pallas kernels  41.2 us (84%)
  local copies, waits for them, and re-layouts  6.96 us (14%)
  between operations  0.65 us (1%)
    pallas_call x1, Pallas kernels, local(): pl.pallas_call(kernel, out_shape=(field, field, jax.ShapeDtypeStruct((27,...  41.2 us
    unnamed x13, local copies, waits for them, and re-layouts  6.96 us

profile of v1, /device:TPU:1, one launch (start us, length us, event | category | flops | bytes accessed | tf_op | source)
XLA Modules:
  0.0 48.8 jit_solution(11216724474688217956)
XLA Ops:
  0.6 0.0 copy-start.4
  0.6 0.6 %copy-done.4 = s32[1,1,27]{2,1,0:T(1,128)S(1)} copy-done((s32[1,1,27]{2,1,0:T(1,128)S(1)}, s32[1,1,27]{2,1,0:T(1,128)}, u32[]{:S(2)}) %copy-start.4) | copy-done | bytes 132
  1.3 0.0 copy-start
  1.3 1.0 %copy-done = bf16[1,1,64,4096]{3,2,1,0:T(8,128)(2,1)S(1)} copy-done((bf16[1,1,64,4096]{3,2,1,0:T(8,128)(2,1)S(1)}, bf16[1,1,64,4096]{3,2,1,0:T(8,128)(2,1)}, u32[]{:S(2)}) %copy-start) | copy-done | bytes 524312
  2.3 0.0 copy-start.1
  2.3 1.0 %copy-done.1 = bf16[1,1,64,4096]{3,2,1,0:T(8,128)(2,1)S(1)} copy-done((bf16[1,1,64,4096]{3,2,1,0:T(8,128)(2,1)S(1)}, bf16[1,1,64,4096]{3,2,1,0:T(8,128)(2,1)}, u32[]{:S(2)}) %copy-start.1) | copy-done | bytes 524312
  3.4 0.0 copy-start.2
  3.4 1.0 %copy-done.2 = bf16[27,64,64]{2,1,0:T(8,128)(2,1)S(1)} copy-done((bf16[27,64,64]{2,1,0:T(8,128)(2,1)S(1)}, bf16[27,64,64]{2,1,0:T(8,128)(2,1)}, u32[]{:S(2)}) %copy-start.2) | copy-done | bytes 221208
  4.4 0.0 copy-start.3
  4.4 0.7 %copy-done.3 = s32[1,1,4096]{2,1,0:T(1,128)S(1)} copy-done((s32[1,1,4096]{2,1,0:T(1,128)S(1)}, s32[1,1,4096]{2,1,0:T(1,128)}, u32[]{:S(2)}) %copy-start.3) | copy-done | bytes 16408
  5.1 41.2 %shard_map.76 = (bf16[64,4096]{1,0:T(8,128)(2,1)S(1)}, bf16[64,4096]{1,0:T(8,128)(2,1)S(1)}, f32[27,64,64]{2,1,0:T(8,128)S(1)}) custom-call(bf16[64,4096]{1,0:T(8,128)(2,1)S(1)} %bitcast.6, bf16[64,4096]{1,0:T(8,128)(2,1)S(1)} %bitcast.7, bf16[27,64,64]{2,1,0:T(8,128)(2,1)S(1)} %copy-done.2, s32[1,27]{1,0:T(1,128)S(1)} %bitcast.11, s32[1,4096]{1,0:T(1,128)S(1)} %bitcast.10), custom_call_target="tpu_custom_call" | custom-call | tf_op jit(solution)/shard_map/pallas_call | solution.py:305
  46.3 0.8 %copy.11 = bf16[1,1,64,4096]{3,2,1,0:T(8,128)(2,1)} copy(bf16[1,1,64,4096]{3,2,1,0:T(8,128)(2,1)S(1)} %bitcast.9) | data formatting | bytes 1048576
  47.1 0.8 %copy.12 = bf16[1,1,64,4096]{3,2,1,0:T(8,128)(2,1)} copy(bf16[1,1,64,4096]{3,2,1,0:T(8,128)(2,1)S(1)} %bitcast.8) | data formatting | bytes 1048576
  47.9 0.9 %copy.13 = f32[27,64,64]{2,1,0:T(8,128)} copy(f32[27,64,64]{2,1,0:T(8,128)S(1)} %get-tuple-element.14) | data formatting | bytes 884736
Async XLA Ops:
  0.6 0.7 %copy-start.4 = (s32[1,1,27]{2,1,0:T(1,128)S(1)}, s32[1,1,27]{2,1,0:T(1,128)}, u32[]{:S(2)}) copy-start(s32[1,1,27]{2,1,0:T(1,128)} %param.8) | copy-start | bytes 328
  1.3 1.0 %copy-start = (bf16[1,1,64,4096]{3,2,1,0:T(8,128)(2,1)S(1)}, bf16[1,1,64,4096]{3,2,1,0:T(8,128)(2,1)}, u32[]{:S(2)}) copy-start(bf16[1,1,64,4096]{3,2,1,0:T(8,128)(2,1)} %param.5) | copy-start | bytes 1572868
  2.3 1.0 %copy-start.1 = (bf16[1,1,64,4096]{3,2,1,0:T(8,128)(2,1)S(1)}, bf16[1,1,64,4096]{3,2,1,0:T(8,128)(2,1)}, u32[]{:S(2)}) copy-start(bf16[1,1,64,4096]{3,2,1,0:T(8,128)(2,1)} %param.6) | copy-start | bytes 1572868
  3.4 1.0 %copy-start.2 = (bf16[27,64,64]{2,1,0:T(8,128)(2,1)S(1)}, bf16[27,64,64]{2,1,0:T(8,128)(2,1)}, u32[]{:S(2)}) copy-start(bf16[27,64,64]{2,1,0:T(8,128)(2,1)} %w_ref.1) | copy-start | bytes 663556
  4.4 0.7 %copy-start.3 = (s32[1,1,4096]{2,1,0:T(1,128)S(1)}, s32[1,1,4096]{2,1,0:T(1,128)}, u32[]{:S(2)}) copy-start(s32[1,1,4096]{2,1,0:T(1,128)} %param.9) | copy-start | bytes 49156

commit v2 on v1

--- a/solution.py
+++ b/solution.py
@@ -30,9 +30,9 @@
 
 
 def kernel(
-    feat_hbm, cot_hbm, w_ref, nb_ref, occ_ref,
-    out_hbm, gin_hbm, gw_ref,
-    feat_v, cot_v, out_v, gin_v, mask_v, s9f, s9u, u3, wf, wb,
+    feat_hbm, cot_hbm, w_hbm, nb_hbm, occ_hbm,
+    out_hbm, gin_hbm, gw_hbm,
+    feat_v, cot_v, w_ref, nb_ref, occ_ref, out_v, gin_v, products, mask_v, s9f, s9u, u3, wf, wb,
     halo_send, halo_recv, part, pair_recv, half, xy_recv, own, z_recv, total, final,
     in_sem, out_sem, halo_ssem, halo_rsem, ar_ssem, ar_rsem,
 ):
@@ -54,8 +54,14 @@
 
     feat_in = pltpu.make_async_copy(feat_hbm, feat_v, in_sem.at[0])
     cot_in = pltpu.make_async_copy(cot_hbm, cot_v, in_sem.at[1])
+    w_in = pltpu.make_async_copy(w_hbm, w_ref, in_sem.at[2])
+    occ_in = pltpu.make_async_copy(occ_hbm, occ_ref, in_sem.at[3])
+    nb_in = pltpu.make_async_copy(nb_hbm, nb_ref, in_sem.at[4])
+    occ_in.start()
     feat_in.start()
     cot_in.start()
+    w_in.start()
+    nb_in.start()
 
     barrier = pltpu.get_barrier_semaphore()
     signals = 0
@@ -69,6 +75,41 @@
         pl.semaphore_signal(barrier, inc=1, device_id=z_peer(j), device_id_type=MESH)
         signals += 1
 
+    def occ_at(z):
+        return occ_ref[:, pl.ds(z * PLANE, PLANE)].astype(F32)
+
+    occ_in.wait()
+    feat_in.wait()
+    for n, z in enumerate((BS - 1, 0)):
+        halo_send[0, n] = (feat_v[:, z * PLANE : (z + 1) * PLANE].astype(F32) * occ_at(z)).astype(BF)
+    pl.semaphore_wait(barrier, signals)
+
+    def halo_copy(field, n):
+        return pltpu.make_async_remote_copy(
+            src_ref=halo_send.at[field, n],
+            dst_ref=halo_recv.at[field, n],
+            send_sem=halo_ssem.at[field, n],
+            recv_sem=halo_rsem.at[field, n],
+            device_id=(up_dev, down_dev)[n],
+            device_id_type=MESH,
+        )
+
+    halos = [[halo_copy(field, n) for n in range(2)] for field in range(2)]
+    halos[0][0].start()
+    halos[0][1].start()
+
+    def fill(s9, plane, layer, slot):
+        lanes = pl.ds(pl.multiple_of(slot * PLANE, PLANE), PLANE)
+        for k, moved in enumerate(spread(plane, x_iota)):
+            s9[k * C : (k + 1) * C, lanes] = moved.astype(BF) * mask_v[layer, k]
+
+    cot_in.wait()
+    for n, z in enumerate((BS - 1, 0)):
+        halo_send[1, n] = (cot_v[:, z * PLANE : (z + 1) * PLANE].astype(F32) * occ_at(z)).astype(BF)
+    halos[1][0].start()
+    halos[1][1].start()
+
+    nb_in.wait()
     lane = lax.broadcasted_iota(jnp.int32, (C, PLANE), 1)
     x_iota = lane % BS
     y_iota = lane // BS
@@ -86,40 +127,6 @@
                 outer = jnp.where(x_out, at(dy, dx), at(dy, 0))
                 mask_v[layer, 3 * (dy + 1) + dx + 1] = jnp.where(y_out, outer, inner).astype(BF)
 
-    def occ_at(z):
-        return occ_ref[:, pl.ds(z * PLANE, PLANE)].astype(F32)
-
-    feat_in.wait()
-    for n, z in enumerate((BS - 1, 0)):
-        halo_send[0, n] = (feat_v[:, z * PLANE : (z + 1) * PLANE].astype(F32) * occ_at(z)).astype(BF)
-    pl.semaphore_wait(barrier, signals)
-
-    def halo_copy(field, n):
-        return pltpu.make_async_remote_copy(
-            src_ref=halo_send.at[field, n],
-            dst_ref=halo_recv.at[field, n],
-            send_sem=halo_ssem.at[field, n],
-            recv_sem=halo_rsem.at[field, n],
-            device_id=(up_dev, down_dev)[n],
-            device_id_type=MESH,
-        )
-
-    halos = [[halo_copy(field, n) for n in range(2)] for field in range(2)]
-    halos[0][0].start()
-    halos[0][1].start()
-
-    def fill(s9, plane, layer, slot):
-        lanes = pl.ds(pl.multiple_of(slot * PLANE, PLANE), PLANE)
-        for k, moved in enumerate(spread(plane, x_iota)):
-            s9[k * C : (k + 1) * C, lanes] = moved.astype(BF) * mask_v[layer, k]
-
-    cot_in.wait()
-    for n, z in enumerate((BS - 1, 0)):
-        halo_send[1, n] = (cot_v[:, z * PLANE : (z + 1) * PLANE].astype(F32) * occ_at(z)).astype(BF)
-    halos[1][0].start()
-    halos[1][1].start()
-
-    u3[...] = jnp.zeros_like(u3)
 
     def own_planes(z, carry):
         z0 = pl.multiple_of(z * PLANE, PLANE)
@@ -131,25 +138,45 @@
             u3[dz * C : (dz + 1) * C, pl.ds(pl.multiple_of((z + dz) * PLANE, PLANE), PLANE)] = ups
         return carry
 
-    lax.fori_loop(0, BS, own_planes, 0)
-
-    halos[0][0].wait_recv()
-    halos[0][1].wait_recv()
-    fill(s9f, halo_recv[0, 0].astype(F32), 0, 0)
-    fill(s9f, halo_recv[0, 1].astype(F32), 2, BS + 1)
-
-    for t in range(3):
-        width = min(PLANE, TAPS * C - t * PLANE)
-        g = lax.dot_general(
-            u3[...], s9f[t * PLANE : t * PLANE + width, :],
-            (((1,), (1,)), ((), ())), preferred_element_type=F32,
-        )
-        for n in range(0, width, 128):
-            for r in range(6):
-                w = min(128, width - n)
-                part[(2 * t + n // 128) * 6 + r, :, 0:w] = g[32 * r : 32 * r + 32, n : n + w]
     part[24:30, :, C:128] = jnp.zeros((6, 32, C), F32)
     part[30:32] = jnp.zeros((2, 32, 128), F32)
+    u3[0:C, V : V + PLANE] = jnp.zeros((C, PLANE), BF)
+    u3[2 * C : 3 * C, PLANE : 2 * PLANE] = jnp.zeros((C, PLANE), BF)
+    lax.fori_loop(0, BS, own_planes, 0)
+
+    def columns(t):
+        return t * PLANE, min(PLANE, TAPS * C - t * PLANE)
+
+    def chunk(t, n, r):
+        return (2 * t + n // 128) * 6 + r
+
+    nt = (((1,), (1,)), ((), ()))
+    for t in range(3):
+        base, width = columns(t)
+        g = lax.dot_general(
+            u3[:, PLANE : PLANE + V], s9f[base : base + width, PLANE : PLANE + V], nt,
+            preferred_element_type=F32,
+        )
+        for n in range(0, width, 128):
+            w = min(128, width - n)
+            for r in range(6):
+                part[chunk(t, n, r), :, 0:w] = g[32 * r : 32 * r + 32, n : n + w]
+
+    for n, layer in ((0, 0), (1, 2)):
+        halos[0][n].wait_recv()
+        slot = layer * (BS + 1) // 2
+        fill(s9f, halo_recv[0, n].astype(F32), layer, slot)
+        edge = u3[layer * C : layer * C + C, slot * PLANE : slot * PLANE + PLANE]
+        for t in range(3):
+            base, width = columns(t)
+            g = lax.dot_general(
+                edge, s9f[base : base + width, slot * PLANE : slot * PLANE + PLANE], nt,
+                preferred_element_type=F32,
+            )
+            for m in range(0, width, 128):
+                w = min(128, width - m)
+                for h in range(2):
+                    part[chunk(t, m, 2 * layer + h), :, 0:w] += g[32 * h : 32 * h + 32, m : m + w]
 
     pair = pltpu.make_async_remote_copy(
         src_ref=part.at[pl.ds((1 - cc) * N_XY, N_XY)],
@@ -161,11 +188,6 @@
     )
     pair.start()
 
-    for k in range(27):
-        dz, j = k // 9, k % 9
-        wf[dz * C : (dz + 1) * C, j * C : (j + 1) * C] = w_ref[k]
-        wb[dz * C : (dz + 1) * C, j * C : (j + 1) * C] = jnp.transpose(w_ref[26 - k].astype(F32)).astype(BF)
-
     pair.wait_recv()
     half[...] = part[pl.ds(cc * N_XY, N_XY)] + pair_recv[...]
 
@@ -185,25 +207,28 @@
     for j in xy_order:
         xy_copies[j].start()
 
+    w_in.wait()
+    for k in range(27):
+        dz, j = k // 9, k % 9
+        wf[dz * C : (dz + 1) * C, j * C : (j + 1) * C] = w_ref[k]
+        wb[dz * C : (dz + 1) * C, j * C : (j + 1) * C] = jnp.transpose(w_ref[26 - k].astype(F32)).astype(BF)
+
     def convolve(weights, s9, dst):
-        def product(slot):
-            return jnp.dot(
-                weights[...], s9[:, pl.ds(pl.multiple_of(slot * PLANE, PLANE), PLANE)],
-                preferred_element_type=F32,
+        step = 6 * PLANE
+        for n in range(0, EXT, step):
+            products[:, n : n + step] = jnp.dot(
+                weights[...], s9[:, n : n + step], preferred_element_type=F32
             )
 
-        first = product(0)
-        second = product(1)
-
-        def step(z, carry):
-            low, mid = carry
-            r = product(z + 2)
+        def combine(z, carry):
             z0 = pl.multiple_of(z * PLANE, PLANE)
-            occ = occ_ref[:, pl.ds(z0, PLANE)].astype(F32)
-            dst[:, pl.ds(z0, PLANE)] = ((mid + r[2 * C :]) * occ).astype(BF)
-            return r[:C], low + r[C : 2 * C]
-
-        lax.fori_loop(0, BS, step, (second[:C], first[:C] + second[C : 2 * C]))
+            acc = products[0:C, pl.ds(z0, PLANE)]
+            for dz in (1, 2):
+                acc += products[dz * C : dz * C + C, pl.ds(pl.multiple_of(z0 + dz * PLANE, PLANE), PLANE)]
+            dst[:, pl.ds(z0, PLANE)] = (acc * occ_ref[:, pl.ds(z0, PLANE)].astype(F32)).astype(BF)
+            return carry
+
+        lax.fori_loop(0, BS, combine, 0)
 
     convolve(wf, s9f, out_v)
     out_copy = pltpu.make_async_copy(out_v, out_hbm, out_sem.at[0])
@@ -267,25 +292,28 @@
     for j in xy_order:
         back_copies[j].start()
     final[cc * N_XY + xy] = total[...]
-    for j in xy_order:
+
+    def forward(i):
+        slot = final.at[cc * N_XY + i]
+        copy = pltpu.make_async_remote_copy(
+            src_ref=slot, dst_ref=slot, send_sem=ar_ssem.at[40 + i], recv_sem=ar_rsem.at[40 + i],
+            device_id=pair_dev, device_id_type=MESH,
+        )
+        copy.start()
+        return copy
+
+    forwards = [forward(xy)]
+    for j in reversed(xy_order):
         back_copies[j].wait_recv()
-    last = pltpu.make_async_remote_copy(
-        src_ref=final.at[pl.ds(cc * N_XY, N_XY)],
-        dst_ref=final.at[pl.ds(cc * N_XY, N_XY)],
-        send_sem=ar_ssem.at[40],
-        recv_sem=ar_rsem.at[40],
-        device_id=pair_dev,
-        device_id_type=MESH,
-    )
-    last.start()
-    last.wait_recv()
-    for k in range(27):
-        dz, j = k // 9, k % 9
-        for h in range(2):
-            gw_ref[k, 32 * h : 32 * h + 32, :] = final[(j // 2) * 6 + 2 * dz + h, :, (j % 2) * C : (j % 2 + 1) * C]
+        forwards.append(forward(lax.rem(xy + N_XY - j, N_XY)))
+    for copy in forwards:
+        copy.wait_recv()
+    gw_copy = pltpu.make_async_copy(final, gw_hbm, out_sem.at[2])
+    gw_copy.start()
 
     pair.wait_send()
-    last.wait_send()
+    for copy in forwards:
+        copy.wait_send()
     for j in xy_order:
         xy_copies[j].wait_send()
         back_copies[j].wait_send()
@@ -296,22 +324,47 @@
             halos[field][n].wait_send()
     out_copy.wait()
     gin_copy.wait()
+    gw_copy.wait()
+
+
+def deliver(out_ref, gin_ref, final_ref, out_hbm, gin_hbm, gw_hbm, final_v, gw_v, sems):
+    copies = [
+        pltpu.make_async_copy(final_ref, final_v, sems.at[0]),
+        pltpu.make_async_copy(out_ref, out_hbm, sems.at[1]),
+        pltpu.make_async_copy(gin_ref, gin_hbm, sems.at[2]),
+    ]
+    for copy in copies:
+        copy.start()
+    copies[0].wait()
+    for k in range(27):
+        dz, j = k // 9, k % 9
+        for h in range(2):
+            gw_v[k, 32 * h : 32 * h + 32, :] = final_v[(j // 2) * 6 + 2 * dz + h, :, (j % 2) * C : (j % 2 + 1) * C]
+    gw_copy = pltpu.make_async_copy(gw_v, gw_hbm, sems.at[3])
+    gw_copy.start()
+    copies[1].wait()
+    copies[2].wait()
+    gw_copy.wait()
 
 
 def local(features, cotangent, weight, neighbours, occupancy):
-    vmem = pl.BlockSpec(memory_space=pltpu.VMEM)
+    hbm = pl.BlockSpec(memory_space=pltpu.HBM)
     anywhere = pl.BlockSpec(memory_space=pl.ANY)
     field = jax.ShapeDtypeStruct((C, V), BF)
-    output, grad_input, grad_weight = pl.pallas_call(
+    output, grad_input, chunks = pl.pallas_call(
         kernel,
-        out_shape=(field, field, jax.ShapeDtypeStruct((27, C, C), F32)),
-        in_specs=[anywhere, anywhere, vmem, pl.BlockSpec(memory_space=pltpu.SMEM), vmem],
-        out_specs=(anywhere, anywhere, vmem),
+        out_shape=(field, field, jax.ShapeDtypeStruct((32, 32, 128), F32)),
+        in_specs=[hbm, hbm, hbm, hbm, hbm],
+        out_specs=(anywhere, anywhere, anywhere),
         scratch_shapes=[
             pltpu.VMEM((C, V), BF),
             pltpu.VMEM((C, V), BF),
+            pltpu.VMEM((27, C, C), BF),
+            pltpu.SMEM((1, 27), jnp.int32),
+            pltpu.VMEM((1, V), jnp.int32),
             pltpu.VMEM((C, V), BF),
             pltpu.VMEM((C, V), BF),
+            pltpu.VMEM((3 * C, EXT), F32),
             pltpu.VMEM((3, TAPS, C, PLANE), BF),
             pltpu.VMEM((TAPS * C, EXT), BF),
             pltpu.VMEM((TAPS * C, EXT), BF),
@@ -328,20 +381,35 @@
             pltpu.VMEM((8, 32, 128), F32),
             pltpu.VMEM((32, 128), F32),
             pltpu.VMEM((32, 32, 128), F32),
-            pltpu.SemaphoreType.DMA((2,)),
-            pltpu.SemaphoreType.DMA((2,)),
+            pltpu.SemaphoreType.DMA((5,)),
+            pltpu.SemaphoreType.DMA((3,)),
             pltpu.SemaphoreType.DMA((2, 2)),
             pltpu.SemaphoreType.DMA((2, 2)),
-            pltpu.SemaphoreType.DMA((41,)),
-            pltpu.SemaphoreType.DMA((41,)),
+            pltpu.SemaphoreType.DMA((56,)),
+            pltpu.SemaphoreType.DMA((56,)),
         ],
         compiler_params=pltpu.CompilerParams(
-            collective_id=0, has_side_effects=True, vmem_limit_bytes=50 * 2**20
+            collective_id=0, has_side_effects=True, vmem_limit_bytes=40 * 2**20
         ),
     )(
-        features.reshape(C, V), cotangent.reshape(C, V), weight,
-        neighbours.reshape(1, 27), occupancy.reshape(1, V),
+        pltpu.with_memory_space_constraint(features.reshape(C, V), pltpu.HBM),
+        pltpu.with_memory_space_constraint(cotangent.reshape(C, V), pltpu.HBM),
+        pltpu.with_memory_space_constraint(weight, pltpu.HBM),
+        pltpu.with_memory_space_constraint(neighbours.reshape(1, 27), pltpu.HBM),
+        pltpu.with_memory_space_constraint(occupancy.reshape(1, V), pltpu.HBM),
     )
+    output, grad_input, grad_weight = pl.pallas_call(
+        deliver,
+        out_shape=(field, field, jax.ShapeDtypeStruct((27, C, C), F32)),
+        in_specs=[anywhere, anywhere, anywhere],
+        out_specs=(hbm, hbm, hbm),
+        scratch_shapes=[
+            pltpu.VMEM((32, 32, 128), F32),
+            pltpu.VMEM((27, C, C), F32),
+            pltpu.SemaphoreType.DMA((4,)),
+        ],
+        compiler_params=pltpu.CompilerParams(vmem_limit_bytes=16 * 2**20),
+    )(output, grad_input, chunks)
     return output.reshape(1, 1, C, V), grad_input.reshape(1, 1, C, V), grad_weight
 
 

time: 49.1 us -> 40.9 us (0.83)
  local copies, waits for them, and re-layouts: 6.96 us -> 0 us
  Pallas kernels: 41.2 us -> 40 us
    unnamed x13 -> x0, local copies, waits for them, and re-layouts: 6.96 us -> none
    pallas_call x1 -> x2, Pallas kernels: 41.2 us -> 40 us  [the longest x1 38.7 us: local(): pl.pallas_call(kernel, out_shape=(field, field, jax.ShapeDtypeStruct((32,...]
where the time goes in v2:
time: 40.9 us; the launch traced here: 40.7 us
  Pallas kernels  40 us (98%)
  between operations  0.64 us (2%)
    pallas_call x1, Pallas kernels, local(): pl.pallas_call(kernel, out_shape=(field, field, jax.ShapeDtypeStruct((32,...  38.7 us
    pallas_call x1, Pallas kernels, local(): pl.pallas_call(deliver, out_shape=(field, field, jax.ShapeDtypeStruct((27...  1.33 us

profile of v2, /device:TPU:1, one launch (start us, length us, event | category | flops | bytes accessed | tf_op | source)
XLA Modules:
  0.0 40.7 jit_solution(1625808121858376101)
XLA Ops:
  0.6 38.7 %shard_map.76 = (bf16[64,4096]{1,0:T(8,128)(2,1)S(1)}, bf16[64,4096]{1,0:T(8,128)(2,1)S(1)}, f32[32,32,128]{2,1,0:T(8,128)S(1)}) custom-call(bf16[64,4096]{1,0:T(8,128)(2,1)} %bitcast.6, bf16[64,4096]{1,0:T(8,128)(2,1)} %bitcast.7, bf16[27,64,64]{2,1,0:T(8,128)(2,1)} %w_hbm.1, s32[1,27]{1,0:T(1,128)} %bitcast.9, s32[1,4096]{1,0:T(1,128)} %bitcast.8), custom_call_target="tpu_custom_call" | custom-call | tf_op jit(solution)/shard_map/pallas_call | solution.py:354
  39.4 1.3 %shard_map.77 = (bf16[64,4096]{1,0:T(8,128)(2,1)}, bf16[64,4096]{1,0:T(8,128)(2,1)}, f32[27,64,64]{2,1,0:T(8,128)}) custom-call(bf16[64,4096]{1,0:T(8,128)(2,1)S(1)} %get-tuple-element.9.out_ref, bf16[64,4096]{1,0:T(8,128)(2,1)S(1)} %get-tuple-element.10.gin_ref, f32[32,32,128]{2,1,0:T(8,128)S(1)} %get-tuple-element.11.final_ref), custom_call_target="tpu_custom_call" | custom-call | tf_op jit(solution)/shard_map/pallas_call | solution.py:401

commit v3 on v2

--- a/solution.py
+++ b/solution.py
@@ -31,10 +31,10 @@
 
 def kernel(
     feat_hbm, cot_hbm, w_hbm, nb_hbm, occ_hbm,
-    out_hbm, gin_hbm, gw_hbm,
-    feat_v, cot_v, w_ref, nb_ref, occ_ref, out_v, gin_v, products, mask_v, s9f, s9u, u3, wf, wb,
+    out_hbm, gin_hbm, chunk_ref,
+    feat_v, cot_v, edge_v, w_ref, nb_ref, occ_ref, out_v, gin_v, products, mask_v, s9f, s9u, u3, wf, wb,
     halo_send, halo_recv, part, pair_recv, half, xy_recv, own, z_recv, total, final,
-    in_sem, out_sem, halo_ssem, halo_rsem, ar_ssem, ar_rsem,
+    in_sem, out_sem, halo_ssem, halo_rsem, ar_ssem, ar_rsem, round_sem,
 ):
     scan = lax.axis_index("scan")
     brick = lax.axis_index("brick")
@@ -52,37 +52,48 @@
     def z_peer(j):
         return (scan, lax.rem(cz + j, N_Z) * N_Y + cy)
 
+    def edge_in(hbm, n):
+        lanes = pl.ds((BS - 1) * PLANE * (1 - n), PLANE)
+        return pltpu.make_async_copy(hbm.at[:, lanes], edge_v.at[n], in_sem.at[5 + n])
+
+    edges = [edge_in(feat_hbm, n) for n in range(2)]
     feat_in = pltpu.make_async_copy(feat_hbm, feat_v, in_sem.at[0])
     cot_in = pltpu.make_async_copy(cot_hbm, cot_v, in_sem.at[1])
     w_in = pltpu.make_async_copy(w_hbm, w_ref, in_sem.at[2])
     occ_in = pltpu.make_async_copy(occ_hbm, occ_ref, in_sem.at[3])
     nb_in = pltpu.make_async_copy(nb_hbm, nb_ref, in_sem.at[4])
     occ_in.start()
+    edges[0].start()
+    edges[1].start()
     feat_in.start()
     cot_in.start()
     w_in.start()
     nb_in.start()
 
+    def around(dx, dy, dz):
+        return (
+            lax.rem(cx + dx, N_X) * N_CORE + cc,
+            lax.rem(cz + dz, N_Z) * N_Y + lax.rem(cy + dy, N_Y),
+        )
+
+    x_line = [around(dx, 0, 0) for dx in (2, 1, 3)]
+    y_line = [around(0, dy, 0) for dy in (2, 1, 3)]
+    z_near = [around(0, 0, 1), around(0, 0, N_Z - 1)]
+    z_next = [around(0, 0, 2), around(0, 0, N_Z - 2)]
+
     barrier = pltpu.get_barrier_semaphore()
-    signals = 0
-    for dev in [up_dev, down_dev, pair_dev]:
+    near = x_line + y_line + z_near + [up_dev, down_dev, pair_dev]
+    for dev in near:
         pl.semaphore_signal(barrier, inc=1, device_id=dev, device_id_type=MESH)
-        signals += 1
-    for j in range(1, N_XY):
-        pl.semaphore_signal(barrier, inc=1, device_id=xy_peer(j)[1], device_id_type=MESH)
-        signals += 1
-    for j in range(1, N_Z):
-        pl.semaphore_signal(barrier, inc=1, device_id=z_peer(j), device_id_type=MESH)
-        signals += 1
 
     def occ_at(z):
         return occ_ref[:, pl.ds(z * PLANE, PLANE)].astype(F32)
 
     occ_in.wait()
-    feat_in.wait()
     for n, z in enumerate((BS - 1, 0)):
-        halo_send[0, n] = (feat_v[:, z * PLANE : (z + 1) * PLANE].astype(F32) * occ_at(z)).astype(BF)
-    pl.semaphore_wait(barrier, signals)
+        edges[n].wait()
+        halo_send[0, n] = (edge_v[n].astype(F32) * occ_at(z)).astype(BF)
+    pl.semaphore_wait(barrier, len(near))
 
     def halo_copy(field, n):
         return pltpu.make_async_remote_copy(
@@ -97,12 +108,15 @@
     halos = [[halo_copy(field, n) for n in range(2)] for field in range(2)]
     halos[0][0].start()
     halos[0][1].start()
+    for dev in x_line + z_near:
+        pl.semaphore_signal(round_sem.at[0], inc=1, device_id=dev, device_id_type=MESH)
 
     def fill(s9, plane, layer, slot):
         lanes = pl.ds(pl.multiple_of(slot * PLANE, PLANE), PLANE)
         for k, moved in enumerate(spread(plane, x_iota)):
             s9[k * C : (k + 1) * C, lanes] = moved.astype(BF) * mask_v[layer, k]
 
+    feat_in.wait()
     cot_in.wait()
     for n, z in enumerate((BS - 1, 0)):
         halo_send[1, n] = (cot_v[:, z * PLANE : (z + 1) * PLANE].astype(F32) * occ_at(z)).astype(BF)
@@ -161,6 +175,10 @@
             w = min(128, width - n)
             for r in range(6):
                 part[chunk(t, n, r), :, 0:w] = g[32 * r : 32 * r + 32, n : n + w]
+
+    pl.semaphore_wait(round_sem.at[0], len(x_line) + len(z_near))
+    for dev in z_next:
+        pl.semaphore_signal(round_sem.at[1], inc=1, device_id=dev, device_id_type=MESH)
 
     for n, layer in ((0, 0), (1, 2)):
         halos[0][n].wait_recv()
@@ -250,6 +268,7 @@
             device_id_type=MESH,
         )
 
+    pl.semaphore_wait(round_sem.at[1], len(z_next))
     z_order = [4, 3, 5, 2, 6, 1, 7]
     z_copies = {j: z_copy(j) for j in z_order}
     for j in z_order:
@@ -302,17 +321,20 @@
         copy.start()
         return copy
 
-    forwards = [forward(xy)]
+    forwards = {0: forward(xy)}
+    chunk_ref[cc * N_XY + xy] = total[...]
     for j in reversed(xy_order):
         back_copies[j].wait_recv()
-        forwards.append(forward(lax.rem(xy + N_XY - j, N_XY)))
-    for copy in forwards:
+        i = lax.rem(xy + N_XY - j, N_XY)
+        forwards[j] = forward(i)
+        chunk_ref[cc * N_XY + i] = final[cc * N_XY + i]
+    for j, copy in forwards.items():
         copy.wait_recv()
-    gw_copy = pltpu.make_async_copy(final, gw_hbm, out_sem.at[2])
-    gw_copy.start()
+    other = pl.ds((1 - cc) * N_XY, N_XY)
+    chunk_ref[other] = final[other]
 
     pair.wait_send()
-    for copy in forwards:
+    for copy in forwards.values():
         copy.wait_send()
     for j in xy_order:
         xy_copies[j].wait_send()
@@ -324,41 +346,40 @@
             halos[field][n].wait_send()
     out_copy.wait()
     gin_copy.wait()
-    gw_copy.wait()
-
-
-def deliver(out_ref, gin_ref, final_ref, out_hbm, gin_hbm, gw_hbm, final_v, gw_v, sems):
+
+
+def deliver(out_ref, gin_ref, chunk_ref, out_hbm, gin_hbm, gw_hbm, gw_v, sems):
     copies = [
-        pltpu.make_async_copy(final_ref, final_v, sems.at[0]),
-        pltpu.make_async_copy(out_ref, out_hbm, sems.at[1]),
-        pltpu.make_async_copy(gin_ref, gin_hbm, sems.at[2]),
+        pltpu.make_async_copy(out_ref, out_hbm, sems.at[0]),
+        pltpu.make_async_copy(gin_ref, gin_hbm, sems.at[1]),
     ]
     for copy in copies:
         copy.start()
-    copies[0].wait()
     for k in range(27):
         dz, j = k // 9, k % 9
         for h in range(2):
-            gw_v[k, 32 * h : 32 * h + 32, :] = final_v[(j // 2) * 6 + 2 * dz + h, :, (j % 2) * C : (j % 2 + 1) * C]
-    gw_copy = pltpu.make_async_copy(gw_v, gw_hbm, sems.at[3])
+            gw_v[k, 32 * h : 32 * h + 32, :] = chunk_ref[(j // 2) * 6 + 2 * dz + h, :, (j % 2) * C : (j % 2 + 1) * C]
+    gw_copy = pltpu.make_async_copy(gw_v, gw_hbm, sems.at[2])
     gw_copy.start()
-    copies[1].wait()
-    copies[2].wait()
+    for copy in copies:
+        copy.wait()
     gw_copy.wait()
 
 
 def local(features, cotangent, weight, neighbours, occupancy):
     hbm = pl.BlockSpec(memory_space=pltpu.HBM)
+    vmem = pl.BlockSpec(memory_space=pltpu.VMEM)
     anywhere = pl.BlockSpec(memory_space=pl.ANY)
     field = jax.ShapeDtypeStruct((C, V), BF)
     output, grad_input, chunks = pl.pallas_call(
         kernel,
         out_shape=(field, field, jax.ShapeDtypeStruct((32, 32, 128), F32)),
         in_specs=[hbm, hbm, hbm, hbm, hbm],
-        out_specs=(anywhere, anywhere, anywhere),
+        out_specs=(anywhere, anywhere, vmem),
         scratch_shapes=[
             pltpu.VMEM((C, V), BF),
             pltpu.VMEM((C, V), BF),
+            pltpu.VMEM((2, C, PLANE), BF),
             pltpu.VMEM((27, C, C), BF),
             pltpu.SMEM((1, 27), jnp.int32),
             pltpu.VMEM((1, V), jnp.int32),
@@ -381,12 +402,13 @@
             pltpu.VMEM((8, 32, 128), F32),
             pltpu.VMEM((32, 128), F32),
             pltpu.VMEM((32, 32, 128), F32),
-            pltpu.SemaphoreType.DMA((5,)),
+            pltpu.SemaphoreType.DMA((7,)),
             pltpu.SemaphoreType.DMA((3,)),
             pltpu.SemaphoreType.DMA((2, 2)),
             pltpu.SemaphoreType.DMA((2, 2)),
             pltpu.SemaphoreType.DMA((56,)),
             pltpu.SemaphoreType.DMA((56,)),
+            pltpu.SemaphoreType.REGULAR((2,)),
         ],
         compiler_params=pltpu.CompilerParams(
             collective_id=0, has_side_effects=True, vmem_limit_bytes=40 * 2**20
@@ -401,12 +423,11 @@
     output, grad_input, grad_weight = pl.pallas_call(
         deliver,
         out_shape=(field, field, jax.ShapeDtypeStruct((27, C, C), F32)),
-        in_specs=[anywhere, anywhere, anywhere],
+        in_specs=[anywhere, anywhere, vmem],
         out_specs=(hbm, hbm, hbm),
         scratch_shapes=[
-            pltpu.VMEM((32, 32, 128), F32),
             pltpu.VMEM((27, C, C), F32),
-            pltpu.SemaphoreType.DMA((4,)),
+            pltpu.SemaphoreType.DMA((3,)),
         ],
         compiler_params=pltpu.CompilerParams(vmem_limit_bytes=16 * 2**20),
     )(output, grad_input, chunks)

time: 40.9 us -> 40.2 us (0.983)
  Pallas kernels: 40 us -> 39.4 us
    pallas_call x1, Pallas kernels: 38.7 us -> 38.1 us  [local(): pl.pallas_call(kernel, out_shape=(field, field, jax.ShapeDtypeStruct((32,...]
where the time goes in v3:
time: 40.2 us; the launch traced here: 40 us
  Pallas kernels  39.4 us (98%)
  between operations  0.64 us (2%)
    pallas_call x1, Pallas kernels, local(): pl.pallas_call(kernel, out_shape=(field, field, jax.ShapeDtypeStruct((32,...  38.1 us
    pallas_call x1, Pallas kernels, local(): pl.pallas_call(deliver, out_shape=(field, field, jax.ShapeDtypeStruct((27...  1.29 us

profile of v3, /device:TPU:1, one launch (start us, length us, event | category | flops | bytes accessed | tf_op | source)
XLA Modules:
  0.0 40.0 jit_solution(5857059113695816640)
XLA Ops:
  0.6 38.1 %shard_map.76 = (bf16[64,4096]{1,0:T(8,128)(2,1)S(1)}, bf16[64,4096]{1,0:T(8,128)(2,1)S(1)}, f32[32,32,128]{2,1,0:T(8,128)S(1)}) custom-call(bf16[64,4096]{1,0:T(8,128)(2,1)} %bitcast.6, bf16[64,4096]{1,0:T(8,128)(2,1)} %bitcast.7, bf16[27,64,64]{2,1,0:T(8,128)(2,1)} %w_hbm.1, s32[1,27]{1,0:T(1,128)} %bitcast.9, s32[1,4096]{1,0:T(1,128)} %bitcast.8), custom_call_target="tpu_custom_call" | custom-call | tf_op jit(solution)/shard_map/pallas_call | solution.py:374
  38.8 1.3 %shard_map.77 = (bf16[64,4096]{1,0:T(8,128)(2,1)}, bf16[64,4096]{1,0:T(8,128)(2,1)}, f32[27,64,64]{2,1,0:T(8,128)}) custom-call(bf16[64,4096]{1,0:T(8,128)(2,1)S(1)} %get-tuple-element.9.out_ref, bf16[64,4096]{1,0:T(8,128)(2,1)S(1)} %get-tuple-element.10.gin_ref, f32[32,32,128]{2,1,0:T(8,128)S(1)} %get-tuple-element.11.chunk_ref), custom_call_target="tpu_custom_call" | custom-call | tf_op jit(solution)/shard_map/pallas_call | solution.py:423

commit v4 on v3

--- a/solution.py
+++ b/solution.py
@@ -17,6 +17,11 @@
 N_CORE, N_X, N_Y, N_Z = 2, 4, 4, 8
 N_BRICK = N_Y * N_Z
 N_XY = N_X * N_Y
+UNROLL = 4
+SUBS = 1
+SUB = 32 // SUBS
+UP_SPLIT = 16
+EARLY = 4
 
 
 def spread(plane, x_iota):
@@ -34,7 +39,7 @@
     out_hbm, gin_hbm, chunk_ref,
     feat_v, cot_v, edge_v, w_ref, nb_ref, occ_ref, out_v, gin_v, products, mask_v, s9f, s9u, u3, wf, wb,
     halo_send, halo_recv, part, pair_recv, half, xy_recv, own, z_recv, total, final,
-    in_sem, out_sem, halo_ssem, halo_rsem, ar_ssem, ar_rsem, round_sem,
+    in_sem, out_sem, halo_ssem, halo_rsem, pair_ssem, pair_rsem, xy_ssem, xy_rsem, z_ssem, z_rsem, back_ssem, back_rsem, on_ssem, on_rsem, round_sem,
 ):
     scan = lax.axis_index("scan")
     brick = lax.axis_index("brick")
@@ -65,7 +70,7 @@
     occ_in.start()
     edges[0].start()
     edges[1].start()
-    feat_in.start()
+
     cot_in.start()
     w_in.start()
     nb_in.start()
@@ -82,10 +87,10 @@
     z_next = [around(0, 0, 2), around(0, 0, N_Z - 2)]
 
     barrier = pltpu.get_barrier_semaphore()
-    near = x_line + y_line + z_near + [up_dev, down_dev, pair_dev]
+    near = [up_dev, down_dev, pair_dev] + x_line + y_line + z_near
     for dev in near:
         pl.semaphore_signal(barrier, inc=1, device_id=dev, device_id_type=MESH)
-
+    feat_in.start()
     def occ_at(z):
         return occ_ref[:, pl.ds(z * PLANE, PLANE)].astype(F32)
 
@@ -93,7 +98,6 @@
     for n, z in enumerate((BS - 1, 0)):
         edges[n].wait()
         halo_send[0, n] = (edge_v[n].astype(F32) * occ_at(z)).astype(BF)
-    pl.semaphore_wait(barrier, len(near))
 
     def halo_copy(field, n):
         return pltpu.make_async_remote_copy(
@@ -106,22 +110,10 @@
         )
 
     halos = [[halo_copy(field, n) for n in range(2)] for field in range(2)]
-    halos[0][0].start()
-    halos[0][1].start()
-    for dev in x_line + z_near:
-        pl.semaphore_signal(round_sem.at[0], inc=1, device_id=dev, device_id_type=MESH)
-
     def fill(s9, plane, layer, slot):
         lanes = pl.ds(pl.multiple_of(slot * PLANE, PLANE), PLANE)
         for k, moved in enumerate(spread(plane, x_iota)):
             s9[k * C : (k + 1) * C, lanes] = moved.astype(BF) * mask_v[layer, k]
-
-    feat_in.wait()
-    cot_in.wait()
-    for n, z in enumerate((BS - 1, 0)):
-        halo_send[1, n] = (cot_v[:, z * PLANE : (z + 1) * PLANE].astype(F32) * occ_at(z)).astype(BF)
-    halos[1][0].start()
-    halos[1][1].start()
 
     nb_in.wait()
     lane = lax.broadcasted_iota(jnp.int32, (C, PLANE), 1)
@@ -142,7 +134,15 @@
                 mask_v[layer, 3 * (dy + 1) + dx + 1] = jnp.where(y_out, outer, inner).astype(BF)
 
 
-    def own_planes(z, carry):
+    def several(body, first, last):
+        def step(n, carry):
+            for m in range(UNROLL):
+                body(first + n * UNROLL + m)
+            return carry
+
+        lax.fori_loop(0, (last - first) // UNROLL, step, 0)
+
+    def own_plane(z):
         z0 = pl.multiple_of(z * PLANE, PLANE)
         occ = occ_ref[:, pl.ds(z0, PLANE)].astype(F32)
         live = feat_v[:, pl.ds(z0, PLANE)].astype(F32) * occ
@@ -150,13 +150,26 @@
         ups = (cot_v[:, pl.ds(z0, PLANE)].astype(F32) * occ).astype(BF)
         for dz in range(3):
             u3[dz * C : (dz + 1) * C, pl.ds(pl.multiple_of((z + dz) * PLANE, PLANE), PLANE)] = ups
-        return carry
 
     part[24:30, :, C:128] = jnp.zeros((6, 32, C), F32)
     part[30:32] = jnp.zeros((2, 32, 128), F32)
     u3[0:C, V : V + PLANE] = jnp.zeros((C, PLANE), BF)
     u3[2 * C : 3 * C, PLANE : 2 * PLANE] = jnp.zeros((C, PLANE), BF)
-    lax.fori_loop(0, BS, own_planes, 0)
+    feat_in.wait()
+    cot_in.wait()
+    for n, z in enumerate((BS - 1, 0)):
+        halo_send[1, n] = (cot_v[:, z * PLANE : (z + 1) * PLANE].astype(F32) * occ_at(z)).astype(BF)
+
+    several(own_plane, 0, EARLY)
+    pl.semaphore_wait(barrier, len(near))
+    halos[0][0].start()
+    halos[0][1].start()
+    for dev in x_line + z_near:
+        pl.semaphore_signal(round_sem.at[0], inc=1, device_id=dev, device_id_type=MESH)
+    halos[1][0].start()
+    halos[1][1].start()
+    several(own_plane, EARLY, BS)
+
 
     def columns(t):
         return t * PLANE, min(PLANE, TAPS * C - t * PLANE)
@@ -196,34 +209,41 @@
                 for h in range(2):
                     part[chunk(t, m, 2 * layer + h), :, 0:w] += g[32 * h : 32 * h + 32, m : m + w]
 
-    pair = pltpu.make_async_remote_copy(
-        src_ref=part.at[pl.ds((1 - cc) * N_XY, N_XY)],
-        dst_ref=pair_recv,
-        send_sem=ar_ssem.at[0],
-        recv_sem=ar_rsem.at[0],
-        device_id=pair_dev,
-        device_id_type=MESH,
-    )
-    pair.start()
-
-    pair.wait_recv()
-    half[...] = part[pl.ds(cc * N_XY, N_XY)] + pair_recv[...]
-
-    def xy_copy(j):
+    rows = [slice(SUB * s, SUB * s + SUB) for s in range(SUBS)]
+
+    def pair_copy(s):
+        return pltpu.make_async_remote_copy(
+            src_ref=part.at[pl.ds((1 - cc) * N_XY, N_XY), rows[s]],
+            dst_ref=pair_recv.at[:, rows[s]],
+            send_sem=pair_ssem.at[s],
+            recv_sem=pair_rsem.at[s],
+            device_id=pair_dev,
+            device_id_type=MESH,
+        )
+
+    pairs = [pair_copy(s) for s in range(SUBS)]
+    for copy in pairs:
+        copy.start()
+
+    def xy_copy(s, j):
         i, dev = xy_peer(j)
         return pltpu.make_async_remote_copy(
-            src_ref=half.at[i],
-            dst_ref=xy_recv.at[j],
-            send_sem=ar_ssem.at[j],
-            recv_sem=ar_rsem.at[j],
+            src_ref=half.at[i, rows[s]],
+            dst_ref=xy_recv.at[j, rows[s]],
+            send_sem=xy_ssem.at[s, j],
+            recv_sem=xy_rsem.at[s, j],
             device_id=dev,
             device_id_type=MESH,
         )
 
     xy_order = [10, 9, 11, 6, 7, 5, 14, 8, 2, 13, 3, 1, 15, 4, 12]
-    xy_copies = {j: xy_copy(j) for j in xy_order}
-    for j in xy_order:
-        xy_copies[j].start()
+    xy_copies = []
+    for s in range(SUBS):
+        pairs[s].wait_recv()
+        half[:, rows[s]] = part[pl.ds(cc * N_XY, N_XY), rows[s]] + pair_recv[:, rows[s]]
+        xy_copies.append({j: xy_copy(s, j) for j in xy_order})
+        for copy in xy_copies[s].values():
+            copy.start()
 
     w_in.wait()
     for k in range(27):
@@ -252,95 +272,98 @@
     out_copy = pltpu.make_async_copy(out_v, out_hbm, out_sem.at[0])
     out_copy.start()
 
-    for j in xy_order:
-        xy_copies[j].wait_recv()
-    own[...] = half[xy]
-    for j in range(1, N_XY):
-        own[...] += xy_recv[j]
-
-    def z_copy(j):
+    def up_plane(z):
+        z0 = pl.multiple_of((z + 1) * PLANE, PLANE)
+        fill(s9u, u3[C : 2 * C, pl.ds(z0, PLANE)].astype(F32), 1, z + 1)
+
+    several(up_plane, 0, UP_SPLIT)
+
+    def z_copy(s, j):
         return pltpu.make_async_remote_copy(
-            src_ref=own,
-            dst_ref=z_recv.at[j],
-            send_sem=ar_ssem.at[16 + j],
-            recv_sem=ar_rsem.at[16 + j],
+            src_ref=own.at[rows[s]],
+            dst_ref=z_recv.at[j, rows[s]],
+            send_sem=z_ssem.at[s, j],
+            recv_sem=z_rsem.at[s, j],
             device_id=z_peer(j),
             device_id_type=MESH,
         )
 
     pl.semaphore_wait(round_sem.at[1], len(z_next))
     z_order = [4, 3, 5, 2, 6, 1, 7]
-    z_copies = {j: z_copy(j) for j in z_order}
-    for j in z_order:
-        z_copies[j].start()
+    z_copies = []
+    for s in range(SUBS):
+        acc = half[xy, rows[s]]
+        for j in xy_order:
+            xy_copies[s][j].wait_recv()
+        for j in xy_order:
+            acc += xy_recv[j, rows[s]]
+        own[rows[s]] = acc
+        z_copies.append({j: z_copy(s, j) for j in z_order})
+        for copy in z_copies[s].values():
+            copy.start()
 
     halos[1][0].wait_recv()
     halos[1][1].wait_recv()
     fill(s9u, halo_recv[1, 0].astype(F32), 0, 0)
     fill(s9u, halo_recv[1, 1].astype(F32), 2, BS + 1)
 
-    def up_planes(z, carry):
-        z0 = pl.multiple_of((z + 1) * PLANE, PLANE)
-        fill(s9u, u3[C : 2 * C, pl.ds(z0, PLANE)].astype(F32), 1, z + 1)
-        return carry
-
-    lax.fori_loop(0, BS, up_planes, 0)
+    several(up_plane, UP_SPLIT, BS)
     convolve(wb, s9u, gin_v)
     gin_copy = pltpu.make_async_copy(gin_v, gin_hbm, out_sem.at[1])
     gin_copy.start()
 
-    for j in z_order:
-        z_copies[j].wait_recv()
-    z_recv[0] = own[...]
-    total[...] = z_recv[cz]
-    for s in range(1, N_Z):
-        total[...] += z_recv[lax.rem(cz + N_Z - s, N_Z)]
-
-    def back_copy(j):
+    def back_copy(s, j):
         i, dev = xy_peer(j)
         return pltpu.make_async_remote_copy(
-            src_ref=total,
-            dst_ref=final.at[cc * N_XY + xy],
-            send_sem=ar_ssem.at[24 + j],
-            recv_sem=ar_rsem.at[24 + j],
+            src_ref=total.at[rows[s]],
+            dst_ref=final.at[cc * N_XY + xy, rows[s]],
+            send_sem=back_ssem.at[s, j],
+            recv_sem=back_rsem.at[s, j],
             device_id=dev,
             device_id_type=MESH,
         )
 
-    back_copies = {j: back_copy(j) for j in xy_order}
-    for j in xy_order:
-        back_copies[j].start()
-    final[cc * N_XY + xy] = total[...]
-
-    def forward(i):
-        slot = final.at[cc * N_XY + i]
+    def forward(s, i):
+        slot = final.at[cc * N_XY + i, rows[s]]
         copy = pltpu.make_async_remote_copy(
-            src_ref=slot, dst_ref=slot, send_sem=ar_ssem.at[40 + i], recv_sem=ar_rsem.at[40 + i],
+            src_ref=slot, dst_ref=slot, send_sem=on_ssem.at[s, i], recv_sem=on_rsem.at[s, i],
             device_id=pair_dev, device_id_type=MESH,
         )
         copy.start()
         return copy
 
-    forwards = {0: forward(xy)}
-    chunk_ref[cc * N_XY + xy] = total[...]
-    for j in reversed(xy_order):
-        back_copies[j].wait_recv()
-        i = lax.rem(xy + N_XY - j, N_XY)
-        forwards[j] = forward(i)
-        chunk_ref[cc * N_XY + i] = final[cc * N_XY + i]
-    for j, copy in forwards.items():
+    back_copies, forwards = [], []
+    for s in range(SUBS):
+        for j in z_order:
+            z_copies[s][j].wait_recv()
+        z_recv[0, rows[s]] = own[rows[s]]
+        acc = z_recv[cz, rows[s]]
+        for n in range(1, N_Z):
+            acc += z_recv[lax.rem(cz + N_Z - n, N_Z), rows[s]]
+        total[rows[s]] = acc
+        back_copies.append({j: back_copy(s, j) for j in xy_order})
+        for copy in back_copies[s].values():
+            copy.start()
+        final[cc * N_XY + xy, rows[s]] = acc
+        chunk_ref[cc * N_XY + xy, rows[s]] = acc
+        forwards.append(forward(s, xy))
+    for s in range(SUBS):
+        for j in reversed(xy_order):
+            back_copies[s][j].wait_recv()
+            i = lax.rem(xy + N_XY - j, N_XY)
+            forwards.append(forward(s, i))
+            chunk_ref[cc * N_XY + i, rows[s]] = final[cc * N_XY + i, rows[s]]
+    for copy in forwards:
         copy.wait_recv()
     other = pl.ds((1 - cc) * N_XY, N_XY)
     chunk_ref[other] = final[other]
 
-    pair.wait_send()
-    for copy in forwards.values():
+    for copy in pairs + forwards:
         copy.wait_send()
-    for j in xy_order:
-        xy_copies[j].wait_send()
-        back_copies[j].wait_send()
-    for j in z_order:
-        z_copies[j].wait_send()
+    for s in range(SUBS):
+        for copies in (xy_copies[s], z_copies[s], back_copies[s]):
+            for copy in copies.values():
+                copy.wait_send()
     for field in range(2):
         for n in range(2):
             halos[field][n].wait_send()
@@ -406,8 +429,16 @@
             pltpu.SemaphoreType.DMA((3,)),
             pltpu.SemaphoreType.DMA((2, 2)),
             pltpu.SemaphoreType.DMA((2, 2)),
-            pltpu.SemaphoreType.DMA((56,)),
-            pltpu.SemaphoreType.DMA((56,)),
+            pltpu.SemaphoreType.DMA((SUBS,)),
+            pltpu.SemaphoreType.DMA((SUBS,)),
+            pltpu.SemaphoreType.DMA((SUBS, N_XY)),
+            pltpu.SemaphoreType.DMA((SUBS, N_XY)),
+            pltpu.SemaphoreType.DMA((SUBS, N_Z)),
+            pltpu.SemaphoreType.DMA((SUBS, N_Z)),
+            pltpu.SemaphoreType.DMA((SUBS, N_XY)),
+            pltpu.SemaphoreType.DMA((SUBS, N_XY)),
+            pltpu.SemaphoreType.DMA((SUBS, N_XY)),
+            pltpu.SemaphoreType.DMA((SUBS, N_XY)),
             pltpu.SemaphoreType.REGULAR((2,)),
         ],
         compiler_params=pltpu.CompilerParams(

time: 40.2 us -> 38 us (0.945)
  Pallas kernels: 39.4 us -> 37.2 us
    pallas_call x1, Pallas kernels: 38.1 us -> 35.9 us  [local(): pl.pallas_call(kernel, out_shape=(field, field, jax.ShapeDtypeStruct((32,...]
where the time goes in v4:
time: 38 us; the launch traced here: 37.8 us
  Pallas kernels  37.2 us (98%)
  between operations  0.64 us (2%)
    pallas_call x1, Pallas kernels, local(): pl.pallas_call(kernel, out_shape=(field, field, jax.ShapeDtypeStruct((32,...  35.9 us
    pallas_call x1, Pallas kernels, local(): pl.pallas_call(deliver, out_shape=(field, field, jax.ShapeDtypeStruct((27...  1.29 us

profile of v4, /device:TPU:1, one launch (start us, length us, event | category | flops | bytes accessed | tf_op | source)
XLA Modules:
  0.0 37.8 jit_solution(8158756931044978336)
XLA Ops:
  0.6 35.9 %shard_map.76 = (bf16[64,4096]{1,0:T(8,128)(2,1)S(1)}, bf16[64,4096]{1,0:T(8,128)(2,1)S(1)}, f32[32,32,128]{2,1,0:T(8,128)S(1)}) custom-call(bf16[64,4096]{1,0:T(8,128)(2,1)} %bitcast.6, bf16[64,4096]{1,0:T(8,128)(2,1)} %bitcast.7, bf16[27,64,64]{2,1,0:T(8,128)(2,1)} %w_hbm.1, s32[1,27]{1,0:T(1,128)} %bitcast.9, s32[1,4096]{1,0:T(1,128)} %bitcast.8), custom_call_target="tpu_custom_call" | custom-call | tf_op jit(solution)/shard_map/pallas_call | solution.py:397
  36.5 1.3 %shard_map.77 = (bf16[64,4096]{1,0:T(8,128)(2,1)}, bf16[64,4096]{1,0:T(8,128)(2,1)}, f32[27,64,64]{2,1,0:T(8,128)}) custom-call(bf16[64,4096]{1,0:T(8,128)(2,1)S(1)} %get-tuple-element.9.out_ref, bf16[64,4096]{1,0:T(8,128)(2,1)S(1)} %get-tuple-element.10.gin_ref, f32[32,32,128]{2,1,0:T(8,128)S(1)} %get-tuple-element.11.chunk_ref), custom_call_target="tpu_custom_call" | custom-call | tf_op jit(solution)/shard_map/pallas_call | solution.py:454

commit v5 on v4

--- a/solution.py
+++ b/solution.py
@@ -21,7 +21,7 @@
 SUBS = 1
 SUB = 32 // SUBS
 UP_SPLIT = 16
-EARLY = 4
+GROUP = 2
 
 
 def spread(plane, x_iota):
@@ -37,7 +37,7 @@
 def kernel(
     feat_hbm, cot_hbm, w_hbm, nb_hbm, occ_hbm,
     out_hbm, gin_hbm, chunk_ref,
-    feat_v, cot_v, edge_v, w_ref, nb_ref, occ_ref, out_v, gin_v, products, mask_v, s9f, s9u, u3, wf, wb,
+    feat_v, cot_v, edge_v, w_ref, nb_ref, occ_ref, out_v, gin_v, products, partial, mask_v, s9f, s9u, u3, wf, wb,
     halo_send, halo_recv, part, pair_recv, half, xy_recv, own, z_recv, total, final,
     in_sem, out_sem, halo_ssem, halo_rsem, pair_ssem, pair_rsem, xy_ssem, xy_rsem, z_ssem, z_rsem, back_ssem, back_rsem, on_ssem, on_rsem, round_sem,
 ):
@@ -110,8 +110,11 @@
         )
 
     halos = [[halo_copy(field, n) for n in range(2)] for field in range(2)]
+    def lane_of(plane):
+        return plane * PLANE if isinstance(plane, int) else pl.multiple_of(plane * PLANE, PLANE)
+
     def fill(s9, plane, layer, slot):
-        lanes = pl.ds(pl.multiple_of(slot * PLANE, PLANE), PLANE)
+        lanes = pl.ds(lane_of(slot), PLANE)
         for k, moved in enumerate(spread(plane, x_iota)):
             s9[k * C : (k + 1) * C, lanes] = moved.astype(BF) * mask_v[layer, k]
 
@@ -143,13 +146,16 @@
         lax.fori_loop(0, (last - first) // UNROLL, step, 0)
 
     def own_plane(z):
-        z0 = pl.multiple_of(z * PLANE, PLANE)
+        z0 = lane_of(z)
         occ = occ_ref[:, pl.ds(z0, PLANE)].astype(F32)
-        live = feat_v[:, pl.ds(z0, PLANE)].astype(F32) * occ
-        fill(s9f, live, 1, z + 1)
+        fill(s9f, feat_v[:, pl.ds(z0, PLANE)].astype(F32) * occ, 1, z + 1)
+
+    def up_rows(z):
+        z0 = lane_of(z)
+        occ = occ_ref[:, pl.ds(z0, PLANE)].astype(F32)
         ups = (cot_v[:, pl.ds(z0, PLANE)].astype(F32) * occ).astype(BF)
         for dz in range(3):
-            u3[dz * C : (dz + 1) * C, pl.ds(pl.multiple_of((z + dz) * PLANE, PLANE), PLANE)] = ups
+            u3[dz * C : (dz + 1) * C, pl.ds(lane_of(z + dz), PLANE)] = ups
 
     part[24:30, :, C:128] = jnp.zeros((6, 32, C), F32)
     part[30:32] = jnp.zeros((2, 32, 128), F32)
@@ -160,7 +166,9 @@
     for n, z in enumerate((BS - 1, 0)):
         halo_send[1, n] = (cot_v[:, z * PLANE : (z + 1) * PLANE].astype(F32) * occ_at(z)).astype(BF)
 
-    several(own_plane, 0, EARLY)
+    several(up_rows, 0, BS)
+    for z in range(GROUP):
+        own_plane(z)
     pl.semaphore_wait(barrier, len(near))
     halos[0][0].start()
     halos[0][1].start()
@@ -168,7 +176,6 @@
         pl.semaphore_signal(round_sem.at[0], inc=1, device_id=dev, device_id_type=MESH)
     halos[1][0].start()
     halos[1][1].start()
-    several(own_plane, EARLY, BS)
 
 
     def columns(t):
@@ -178,16 +185,24 @@
         return (2 * t + n // 128) * 6 + r
 
     nt = (((1,), (1,)), ((), ()))
-    for t in range(3):
-        base, width = columns(t)
-        g = lax.dot_general(
-            u3[:, PLANE : PLANE + V], s9f[base : base + width, PLANE : PLANE + V], nt,
-            preferred_element_type=F32,
-        )
-        for n in range(0, width, 128):
-            w = min(128, width - n)
-            for r in range(6):
-                part[chunk(t, n, r), :, 0:w] = g[32 * r : 32 * r + 32, n : n + w]
+    for first in range(0, BS, GROUP):
+        lanes = slice((first + 1) * PLANE, (first + 1 + GROUP) * PLANE)
+        for t in range(3):
+            base, width = columns(t)
+            g = lax.dot_general(
+                u3[:, lanes], s9f[base : base + width, lanes], nt, preferred_element_type=F32
+            )
+            if first > 0:
+                g += partial[:, base : base + width]
+            if first + GROUP < BS:
+                partial[:, base : base + width] = g
+                continue
+            for n in range(0, width, 128):
+                w = min(128, width - n)
+                for r in range(6):
+                    part[chunk(t, n, r), :, 0:w] = g[32 * r : 32 * r + 32, n : n + w]
+        for z in range(first + GROUP, min(first + 2 * GROUP, BS)):
+            own_plane(z)
 
     pl.semaphore_wait(round_sem.at[0], len(x_line) + len(z_near))
     for dev in z_next:
@@ -409,6 +424,7 @@
             pltpu.VMEM((C, V), BF),
             pltpu.VMEM((C, V), BF),
             pltpu.VMEM((3 * C, EXT), F32),
+            pltpu.VMEM((3 * C, TAPS * C), F32),
             pltpu.VMEM((3, TAPS, C, PLANE), BF),
             pltpu.VMEM((TAPS * C, EXT), BF),
             pltpu.VMEM((TAPS * C, EXT), BF),

time: 38 us -> 37.4 us (0.984)
  Pallas kernels: 37.2 us -> 36.6 us
    pallas_call x1, Pallas kernels: 35.9 us -> 35.3 us  [local(): pl.pallas_call(kernel, out_shape=(field, field, jax.ShapeDtypeStruct((32,...]
where the time goes in v5:
time: 37.4 us; the launch traced here: 37.2 us
  Pallas kernels  36.6 us (98%)
  between operations  0.64 us (2%)
    pallas_call x1, Pallas kernels, local(): pl.pallas_call(kernel, out_shape=(field, field, jax.ShapeDtypeStruct((32,...  35.3 us
    pallas_call x1, Pallas kernels, local(): pl.pallas_call(deliver, out_shape=(field, field, jax.ShapeDtypeStruct((27...  1.29 us

profile of v5, /device:TPU:1, one launch (start us, length us, event | category | flops | bytes accessed | tf_op | source)
XLA Modules:
  0.0 37.2 jit_solution(14767709675958263452)
XLA Ops:
  0.6 35.3 %shard_map.76 = (bf16[64,4096]{1,0:T(8,128)(2,1)S(1)}, bf16[64,4096]{1,0:T(8,128)(2,1)S(1)}, f32[32,32,128]{2,1,0:T(8,128)S(1)}) custom-call(bf16[64,4096]{1,0:T(8,128)(2,1)} %bitcast.6, bf16[64,4096]{1,0:T(8,128)(2,1)} %bitcast.7, bf16[27,64,64]{2,1,0:T(8,128)(2,1)} %w_hbm.1, s32[1,27]{1,0:T(1,128)} %bitcast.9, s32[1,4096]{1,0:T(1,128)} %bitcast.8), custom_call_target="tpu_custom_call" | custom-call | tf_op jit(solution)/shard_map/pallas_call | solution.py:412
  36.0 1.3 %shard_map.77 = (bf16[64,4096]{1,0:T(8,128)(2,1)}, bf16[64,4096]{1,0:T(8,128)(2,1)}, f32[27,64,64]{2,1,0:T(8,128)}) custom-call(bf16[64,4096]{1,0:T(8,128)(2,1)S(1)} %get-tuple-element.9.out_ref, bf16[64,4096]{1,0:T(8,128)(2,1)S(1)} %get-tuple-element.10.gin_ref, f32[32,32,128]{2,1,0:T(8,128)S(1)} %get-tuple-element.11.chunk_ref), custom_call_target="tpu_custom_call" | custom-call | tf_op jit(solution)/shard_map/pallas_call | solution.py:470

commit v6 on v5

--- a/solution.py
+++ b/solution.py
@@ -1,3 +1,5 @@
+import functools
+
 import jax
 import jax.numpy as jnp
 from jax import lax
@@ -24,6 +26,13 @@
 GROUP = 2
 
 
+OWNERS = 14
+
+
+def slot_of(chunk):
+    return chunk if chunk < OWNERS else chunk - OWNERS + N_XY
+
+
 def spread(plane, x_iota):
     left = jnp.where(x_iota == 0, pltpu.roll(plane, PLANE - 15, 1), pltpu.roll(plane, 1, 1))
     right = jnp.where(x_iota == BS - 1, pltpu.roll(plane, 15, 1), pltpu.roll(plane, PLANE - 1, 1))
@@ -157,8 +166,8 @@
         for dz in range(3):
             u3[dz * C : (dz + 1) * C, pl.ds(lane_of(z + dz), PLANE)] = ups
 
-    part[24:30, :, C:128] = jnp.zeros((6, 32, C), F32)
-    part[30:32] = jnp.zeros((2, 32, 128), F32)
+    for n in (14, 15, 29, 30, 31):
+        part[n] = jnp.zeros((32, 128), F32)
     u3[0:C, V : V + PLANE] = jnp.zeros((C, PLANE), BF)
     u3[2 * C : 3 * C, PLANE : 2 * PLANE] = jnp.zeros((C, PLANE), BF)
     feat_in.wait()
@@ -181,8 +190,10 @@
     def columns(t):
         return t * PLANE, min(PLANE, TAPS * C - t * PLANE)
 
-    def chunk(t, n, r):
-        return (2 * t + n // 128) * 6 + r
+    def place(t, n, r):
+        if t < 2:
+            return slot_of((2 * t + n // 128) * 6 + r), slice(0, 128)
+        return slot_of(24 + r // 2), slice(C * (r % 2), C * (r % 2) + C)
 
     nt = (((1,), (1,)), ((), ()))
     for first in range(0, BS, GROUP):
@@ -200,7 +211,8 @@
             for n in range(0, width, 128):
                 w = min(128, width - n)
                 for r in range(6):
-                    part[chunk(t, n, r), :, 0:w] = g[32 * r : 32 * r + 32, n : n + w]
+                    at, cols = place(t, n, r)
+                    part[at, :, cols] = g[32 * r : 32 * r + 32, n : n + w]
         for z in range(first + GROUP, min(first + 2 * GROUP, BS)):
             own_plane(z)
 
@@ -222,14 +234,15 @@
             for m in range(0, width, 128):
                 w = min(128, width - m)
                 for h in range(2):
-                    part[chunk(t, m, 2 * layer + h), :, 0:w] += g[32 * h : 32 * h + 32, m : m + w]
+                    at, cols = place(t, m, 2 * layer + h)
+                    part[at, :, cols] += g[32 * h : 32 * h + 32, m : m + w]
 
     rows = [slice(SUB * s, SUB * s + SUB) for s in range(SUBS)]
 
     def pair_copy(s):
         return pltpu.make_async_remote_copy(
-            src_ref=part.at[pl.ds((1 - cc) * N_XY, N_XY), rows[s]],
-            dst_ref=pair_recv.at[:, rows[s]],
+            src_ref=part.at[pl.ds((1 - cc) * N_XY, OWNERS), rows[s]],
+            dst_ref=pair_recv.at[0:OWNERS, rows[s]],
             send_sem=pair_ssem.at[s],
             recv_sem=pair_rsem.at[s],
             device_id=pair_dev,
@@ -255,10 +268,10 @@
     xy_copies = []
     for s in range(SUBS):
         pairs[s].wait_recv()
-        half[:, rows[s]] = part[pl.ds(cc * N_XY, N_XY), rows[s]] + pair_recv[:, rows[s]]
+        half[0:OWNERS, rows[s]] = part[pl.ds(cc * N_XY, OWNERS), rows[s]] + pair_recv[0:OWNERS, rows[s]]
         xy_copies.append({j: xy_copy(s, j) for j in xy_order})
-        for copy in xy_copies[s].values():
-            copy.start()
+        for j in xy_order:
+            pl.when(lax.rem(xy + j, N_XY) < OWNERS)(xy_copies[s][j].start)
 
     w_in.wait()
     for k in range(27):
@@ -305,17 +318,20 @@
 
     pl.semaphore_wait(round_sem.at[1], len(z_next))
     z_order = [4, 3, 5, 2, 6, 1, 7]
-    z_copies = []
-    for s in range(SUBS):
-        acc = half[xy, rows[s]]
-        for j in xy_order:
-            xy_copies[s][j].wait_recv()
-        for j in xy_order:
-            acc += xy_recv[j, rows[s]]
-        own[rows[s]] = acc
-        z_copies.append({j: z_copy(s, j) for j in z_order})
-        for copy in z_copies[s].values():
-            copy.start()
+    owner = xy < OWNERS
+    z_copies = [{j: z_copy(s, j) for j in z_order} for s in range(SUBS)]
+
+    @pl.when(owner)
+    def _():
+        for s in range(SUBS):
+            acc = half[xy, rows[s]]
+            for j in xy_order:
+                xy_copies[s][j].wait_recv()
+            for j in xy_order:
+                acc += xy_recv[j, rows[s]]
+            own[rows[s]] = acc
+            for copy in z_copies[s].values():
+                copy.start()
 
     halos[1][0].wait_recv()
     halos[1][1].wait_recv()
@@ -344,41 +360,58 @@
             src_ref=slot, dst_ref=slot, send_sem=on_ssem.at[s, i], recv_sem=on_rsem.at[s, i],
             device_id=pair_dev, device_id_type=MESH,
         )
-        copy.start()
         return copy
 
-    back_copies, forwards = [], []
-    for s in range(SUBS):
-        for j in z_order:
-            z_copies[s][j].wait_recv()
-        z_recv[0, rows[s]] = own[rows[s]]
-        acc = z_recv[cz, rows[s]]
-        for n in range(1, N_Z):
-            acc += z_recv[lax.rem(cz + N_Z - n, N_Z), rows[s]]
-        total[rows[s]] = acc
-        back_copies.append({j: back_copy(s, j) for j in xy_order})
-        for copy in back_copies[s].values():
-            copy.start()
-        final[cc * N_XY + xy, rows[s]] = acc
-        chunk_ref[cc * N_XY + xy, rows[s]] = acc
-        forwards.append(forward(s, xy))
+    back_copies = [{j: back_copy(s, j) for j in xy_order} for s in range(SUBS)]
+    forwards = [{j: forward(s, lax.rem(xy + N_XY - j, N_XY)) for j in range(N_XY)} for s in range(SUBS)]
+
+    @pl.when(owner)
+    def _():
+        for s in range(SUBS):
+            for j in z_order:
+                z_copies[s][j].wait_recv()
+            z_recv[0, rows[s]] = own[rows[s]]
+            acc = z_recv[cz, rows[s]]
+            for n in range(1, N_Z):
+                acc += z_recv[lax.rem(cz + N_Z - n, N_Z), rows[s]]
+            total[rows[s]] = acc
+            for copy in back_copies[s].values():
+                copy.start()
+            final[cc * N_XY + xy, rows[s]] = acc
+            chunk_ref[cc * N_XY + xy, rows[s]] = acc
+            forwards[s][0].start()
+
+    def sender(j):
+        return lax.rem(xy + N_XY - j, N_XY)
+
+    def pass_on(s, j):
+        back_copies[s][j].wait_recv()
+        forwards[s][j].start()
+        chunk_ref[cc * N_XY + sender(j), rows[s]] = final[cc * N_XY + sender(j), rows[s]]
+
     for s in range(SUBS):
         for j in reversed(xy_order):
-            back_copies[s][j].wait_recv()
-            i = lax.rem(xy + N_XY - j, N_XY)
-            forwards.append(forward(s, i))
-            chunk_ref[cc * N_XY + i, rows[s]] = final[cc * N_XY + i, rows[s]]
-    for copy in forwards:
-        copy.wait_recv()
-    other = pl.ds((1 - cc) * N_XY, N_XY)
+            pl.when(sender(j) < OWNERS)(functools.partial(pass_on, s, j))
+    for s in range(SUBS):
+        for j in range(N_XY):
+            pl.when(sender(j) < OWNERS)(forwards[s][j].wait_recv)
+    other = pl.ds((1 - cc) * N_XY, OWNERS)
     chunk_ref[other] = final[other]
 
-    for copy in pairs + forwards:
-        copy.wait_send()
     for s in range(SUBS):
-        for copies in (xy_copies[s], z_copies[s], back_copies[s]):
-            for copy in copies.values():
-                copy.wait_send()
+        pairs[s].wait_send()
+        for j in xy_order:
+            pl.when(lax.rem(xy + j, N_XY) < OWNERS)(xy_copies[s][j].wait_send)
+        for j in range(N_XY):
+            pl.when(sender(j) < OWNERS)(forwards[s][j].wait_send)
+
+    @pl.when(owner)
+    def _():
+        for s in range(SUBS):
+            for copies in (z_copies[s], back_copies[s]):
+                for copy in copies.values():
+                    copy.wait_send()
+
     for field in range(2):
         for n in range(2):
             halos[field][n].wait_send()
@@ -396,7 +429,11 @@
     for k in range(27):
         dz, j = k // 9, k % 9
         for h in range(2):
-            gw_v[k, 32 * h : 32 * h + 32, :] = chunk_ref[(j // 2) * 6 + 2 * dz + h, :, (j % 2) * C : (j % 2 + 1) * C]
+            if j < 8:
+                at, half = slot_of((j // 2) * 6 + 2 * dz + h), j % 2
+            else:
+                at, half = slot_of(24 + dz), h
+            gw_v[k, 32 * h : 32 * h + 32, :] = chunk_ref[at, :, C * half : C * half + C]
     gw_copy = pltpu.make_async_copy(gw_v, gw_hbm, sems.at[2])
     gw_copy.start()
     for copy in copies:

time: 37.4 us -> 36.5 us (0.976)
  Pallas kernels: 36.6 us -> 35.7 us
    pallas_call x1, Pallas kernels: 35.3 us -> 34.4 us  [local(): pl.pallas_call(kernel, out_shape=(field, field, jax.ShapeDtypeStruct((32,...]
where the time goes in v6:
time: 36.5 us; the launch traced here: 36.3 us
  Pallas kernels  35.7 us (98%)
  between operations  0.64 us (2%)
    pallas_call x1, Pallas kernels, local(): pl.pallas_call(kernel, out_shape=(field, field, jax.ShapeDtypeStruct((32,...  34.4 us
    pallas_call x1, Pallas kernels, local(): pl.pallas_call(deliver, out_shape=(field, field, jax.ShapeDtypeStruct((27...  1.29 us

profile of v6, /device:TPU:1, one launch (start us, length us, event | category | flops | bytes accessed | tf_op | source)
XLA Modules:
  0.0 36.3 jit_solution(6866544358824798798)
XLA Ops:
  0.6 34.4 %shard_map.76 = (bf16[64,4096]{1,0:T(8,128)(2,1)S(1)}, bf16[64,4096]{1,0:T(8,128)(2,1)S(1)}, f32[32,32,128]{2,1,0:T(8,128)S(1)}) custom-call(bf16[64,4096]{1,0:T(8,128)(2,1)} %bitcast.6, bf16[64,4096]{1,0:T(8,128)(2,1)} %bitcast.7, bf16[27,64,64]{2,1,0:T(8,128)(2,1)} %w_hbm.1, s32[1,27]{1,0:T(1,128)} %bitcast.9, s32[1,4096]{1,0:T(1,128)} %bitcast.8), custom_call_target="tpu_custom_call" | custom-call | tf_op jit(solution)/shard_map/pallas_call | solution.py:449
  35.0 1.3 %shard_map.77 = (bf16[64,4096]{1,0:T(8,128)(2,1)}, bf16[64,4096]{1,0:T(8,128)(2,1)}, f32[27,64,64]{2,1,0:T(8,128)}) custom-call(bf16[64,4096]{1,0:T(8,128)(2,1)S(1)} %get-tuple-element.9.out_ref, bf16[64,4096]{1,0:T(8,128)(2,1)S(1)} %get-tuple-element.10.gin_ref, f32[32,32,128]{2,1,0:T(8,128)S(1)} %get-tuple-element.11.chunk_ref), custom_call_target="tpu_custom_call" | custom-call | tf_op jit(solution)/shard_map/pallas_call | solution.py:507

commit v7 on v6

--- a/solution.py
+++ b/solution.py
@@ -175,9 +175,6 @@
     for n, z in enumerate((BS - 1, 0)):
         halo_send[1, n] = (cot_v[:, z * PLANE : (z + 1) * PLANE].astype(F32) * occ_at(z)).astype(BF)
 
-    several(up_rows, 0, BS)
-    for z in range(GROUP):
-        own_plane(z)
     pl.semaphore_wait(barrier, len(near))
     halos[0][0].start()
     halos[0][1].start()
@@ -185,6 +182,9 @@
         pl.semaphore_signal(round_sem.at[0], inc=1, device_id=dev, device_id_type=MESH)
     halos[1][0].start()
     halos[1][1].start()
+    several(up_rows, 0, BS)
+    for z in range(GROUP):
+        own_plane(z)
 
 
     def columns(t):
@@ -220,8 +220,9 @@
     for dev in z_next:
         pl.semaphore_signal(round_sem.at[1], inc=1, device_id=dev, device_id_type=MESH)
 
+    halos[0][0].wait_recv()
+    halos[0][1].wait_recv()
     for n, layer in ((0, 0), (1, 2)):
-        halos[0][n].wait_recv()
         slot = layer * (BS + 1) // 2
         fill(s9f, halo_recv[0, n].astype(F32), layer, slot)
         edge = u3[layer * C : layer * C + C, slot * PLANE : slot * PLANE + PLANE]

time: 36.5 us -> 36.2 us (level)
  no operation moved by 1% of the time
where the time goes in v7:
time: 36.2 us; the launch traced here: 36 us
  Pallas kernels  35.4 us (98%)
  between operations  0.64 us (2%)
    pallas_call x1, Pallas kernels, local(): pl.pallas_call(kernel, out_shape=(field, field, jax.ShapeDtypeStruct((32,...  34.1 us
    pallas_call x1, Pallas kernels, local(): pl.pallas_call(deliver, out_shape=(field, field, jax.ShapeDtypeStruct((27...  1.29 us

profile of v7, /device:TPU:1, one launch (start us, length us, event | category | flops | bytes accessed | tf_op | source)
XLA Modules:
  0.0 36.0 jit_solution(7580067767208837474)
XLA Ops:
  0.6 34.1 %shard_map.76 = (bf16[64,4096]{1,0:T(8,128)(2,1)S(1)}, bf16[64,4096]{1,0:T(8,128)(2,1)S(1)}, f32[32,32,128]{2,1,0:T(8,128)S(1)}) custom-call(bf16[64,4096]{1,0:T(8,128)(2,1)} %bitcast.6, bf16[64,4096]{1,0:T(8,128)(2,1)} %bitcast.7, bf16[27,64,64]{2,1,0:T(8,128)(2,1)} %w_hbm.1, s32[1,27]{1,0:T(1,128)} %bitcast.9, s32[1,4096]{1,0:T(1,128)} %bitcast.8), custom_call_target="tpu_custom_call" | custom-call | tf_op jit(solution)/shard_map/pallas_call | solution.py:450
  34.7 1.3 %shard_map.77 = (bf16[64,4096]{1,0:T(8,128)(2,1)}, bf16[64,4096]{1,0:T(8,128)(2,1)}, f32[27,64,64]{2,1,0:T(8,128)}) custom-call(bf16[64,4096]{1,0:T(8,128)(2,1)S(1)} %get-tuple-element.9.out_ref, bf16[64,4096]{1,0:T(8,128)(2,1)S(1)} %get-tuple-element.10.gin_ref, f32[32,32,128]{2,1,0:T(8,128)S(1)} %get-tuple-element.11.chunk_ref), custom_call_target="tpu_custom_call" | custom-call | tf_op jit(solution)/shard_map/pallas_call | solution.py:508

commit v8 on v7

--- a/solution.py
+++ b/solution.py
@@ -170,16 +170,15 @@
         part[n] = jnp.zeros((32, 128), F32)
     u3[0:C, V : V + PLANE] = jnp.zeros((C, PLANE), BF)
     u3[2 * C : 3 * C, PLANE : 2 * PLANE] = jnp.zeros((C, PLANE), BF)
-    feat_in.wait()
-    cot_in.wait()
-    for n, z in enumerate((BS - 1, 0)):
-        halo_send[1, n] = (cot_v[:, z * PLANE : (z + 1) * PLANE].astype(F32) * occ_at(z)).astype(BF)
-
     pl.semaphore_wait(barrier, len(near))
     halos[0][0].start()
     halos[0][1].start()
     for dev in x_line + z_near:
         pl.semaphore_signal(round_sem.at[0], inc=1, device_id=dev, device_id_type=MESH)
+    feat_in.wait()
+    cot_in.wait()
+    for n, z in enumerate((BS - 1, 0)):
+        halo_send[1, n] = (cot_v[:, z * PLANE : (z + 1) * PLANE].astype(F32) * occ_at(z)).astype(BF)
     halos[1][0].start()
     halos[1][1].start()
     several(up_rows, 0, BS)

time: 36.2 us -> 36.2 us (level)
  no operation moved by 1% of the time
where the time goes in v8:
time: 36.2 us; the launch traced here: 36 us
  Pallas kernels  35.4 us (98%)
  between operations  0.64 us (2%)
    pallas_call x1, Pallas kernels, local(): pl.pallas_call(kernel, out_shape=(field, field, jax.ShapeDtypeStruct((32,...  34.1 us
    pallas_call x1, Pallas kernels, local(): pl.pallas_call(deliver, out_shape=(field, field, jax.ShapeDtypeStruct((27...  1.29 us

profile of v8, /device:TPU:1, one launch (start us, length us, event | category | flops | bytes accessed | tf_op | source)
XLA Modules:
  0.0 36.0 jit_solution(13891145620298385625)
XLA Ops:
  0.6 34.1 %shard_map.76 = (bf16[64,4096]{1,0:T(8,128)(2,1)S(1)}, bf16[64,4096]{1,0:T(8,128)(2,1)S(1)}, f32[32,32,128]{2,1,0:T(8,128)S(1)}) custom-call(bf16[64,4096]{1,0:T(8,128)(2,1)} %bitcast.6, bf16[64,4096]{1,0:T(8,128)(2,1)} %bitcast.7, bf16[27,64,64]{2,1,0:T(8,128)(2,1)} %w_hbm.1, s32[1,27]{1,0:T(1,128)} %bitcast.9, s32[1,4096]{1,0:T(1,128)} %bitcast.8), custom_call_target="tpu_custom_call" | custom-call | tf_op jit(solution)/shard_map/pallas_call | solution.py:449
  34.7 1.3 %shard_map.77 = (bf16[64,4096]{1,0:T(8,128)(2,1)}, bf16[64,4096]{1,0:T(8,128)(2,1)}, f32[27,64,64]{2,1,0:T(8,128)}) custom-call(bf16[64,4096]{1,0:T(8,128)(2,1)S(1)} %get-tuple-element.9.out_ref, bf16[64,4096]{1,0:T(8,128)(2,1)S(1)} %get-tuple-element.10.gin_ref, f32[32,32,128]{2,1,0:T(8,128)S(1)} %get-tuple-element.11.chunk_ref), custom_call_target="tpu_custom_call" | custom-call | tf_op jit(solution)/shard_map/pallas_call | solution.py:507
